TPU v7x, 32 devices: a whole 2x2x4 slice. The times are simulated.
32 devices in a mesh: rows: 8 (over z, y), panel: 4 (over x, core).
Axes of the slice: x: 2, y: 2, z: 4, core: 2. Of those that a mesh axis runs over, the one named last changes fastest.
Arguments:
- pair_block: bfloat16 [2048, 16384], P('rows', 'panel'), may hold values from -6 to 6
- resolvent: float32 [16384, 16384], P('panel', 'rows'), may hold values from -0.046875 to 0.046875
- virt_coef: bfloat16 [1024, 11200], P('rows', 'panel'), may hold values from -0.1875 to 0.1875
- slot_row: int32 [2048], replicated, may hold values from 0 to 2047, each once
Outputs:
- backward: float32 [2, 11200, 16384], P(None, 'panel', 'rows')
Inputs may be any that keep to these rules, and one draw needn't show every extreme that they name: `slot_row`: every pair row appears exactly once.
All inputs are finite; a program needn't handle non-finite values.
Results may differ from a plain program's by a relative error of at most 0.0041.
Values may be sent and summed in bfloat16 or wider, within the bound.
No kernel may reach another device: no remote copies, remote signals or barrier semaphores. Data moves between devices by JAX's collectives and lax.ppermute only.
A program may use at most 192 MiB of HBM per device.

v0:
```python
import jax
import jax.numpy as jnp
from jax import lax
from jax.sharding import PartitionSpec as P

OCC_B = 2


def body(pair_block, resolvent, virt_coef, slot_row):
    resolvent_round = resolvent.astype(jnp.bfloat16)
    gathered = None
    partial_sum = jnp.dot(
        lax.all_gather(pair_block, "rows", axis=0, tiled=True),
        resolvent_round,
        preferred_element_type=jnp.float32,
    )
    own_rows = lax.psum_scatter(partial_sum, "panel", scatter_dimension=0, tiled=True).astype(
        jnp.bfloat16
    )
    gathered = lax.all_gather(own_rows, "panel", axis=0, tiled=True)
    grouped = jnp.take(gathered, slot_row, axis=0)
    grouped = grouped.reshape(OCC_B, slot_row.shape[0] // OCC_B, gathered.shape[1])
    coef_all = lax.all_gather(virt_coef, "rows", axis=0, tiled=True)
    return jnp.einsum("am,oac->omc", coef_all, grouped, preferred_element_type=jnp.float32)


def solution(mesh):
    placed = (P("rows", "panel"), P("panel", "rows"), P("rows", "panel"), P())
    return jax.shard_map(
        body, mesh=mesh, in_specs=placed, out_specs=P(None, "panel", "rows"), check_vma=False
    )
```

profile of v0, /device:TPU:0, one launch (start us, length us, event | category | flops | bytes accessed | tf_op | source)
XLA Modules:
  0.0 606.9 jit_solution(7234466197821076055)
XLA Ops:
  6.5 0.0 all-gather.4.cloned.1.call-start
  6.5 0.7 all-gather.4.cloned.1.call-update
  7.3 0.0 reduce-scatter.2.cloned.1.call-start
  7.3 232.5 %all-gather.4.cloned.1.call-done = bf16[2048,4096]{1,0:T(8,128)(2,1)} async-done(((bf16[256,4096]{1,0:T(8,128)(2,1)}), bf16[2048,4096]{1,0:T(8,128)(2,1)}) %all-gather.4.cloned.1.call-update) | async-done | bytes 16777232 | tf_op jit(solution)/shard_map/all_gather | solution.py:13
  239.8 45.8 %fusion = f32[2048,2048]{1,0:T(8,128)} fusion(bf16[2048,4096]{1,0:T(8,128)(2,1)} %all-gather.4.cloned.1.call-done, f32[4096,2048]{1,0:T(8,128)} %param.5), kind=kOutput, calls=%fused_computation.2 | convolution fusion | flops 34368126976 | bytes 67108864 | tf_op jit(solution)/shard_map/dot_general | solution.py:12
  285.6 0.0 reduce-scatter.2.cloned.1.call-update
  285.7 0.0 copy-start
  285.7 0.0 all-gather.6.cloned.1.call-start
  285.7 124.4 %reduce-scatter.2.cloned.1.call-done = f32[512,2048]{1,0:T(8,128)} async-done(((f32[2048,2048]{1,0:T(8,128)}), f32[512,2048]{1,0:T(8,128)}) %reduce-scatter.2.cloned.1.call-update) | async-done | bytes 4194320 | tf_op jit(solution)/shard_map/reduce_scatter | solution.py:17
  410.1 3.8 convert_element_type.7
  413.9 0.0 all-gather.6.cloned.1.call-update
  414.0 0.2 all-gather.8.cloned.1.call-start
  414.2 0.3 all-gather.8.cloned.1.call-update
  414.6 0.0 copy-done
  414.6 57.8 %all-gather.6.cloned.1.call-done = bf16[2048,2048]{1,0:T(8,128)(2,1)} async-done(((bf16[512,2048]{1,0:T(8,128)(2,1)}), bf16[2048,2048]{1,0:T(8,128)(2,1)}) %all-gather.6.cloned.1.call-update) | async-done | bytes 8388624 | tf_op jit(solution)/shard_map/all_gather | solution.py:20
  472.4 20.8 %gather_fusion = bf16[2048,2048]{1,0:T(8,128)(2,1)} fusion(bf16[2048,2048]{1,0:T(8,128)(2,1)} %all-gather.6.cloned.1.call-done, s32[2048]{0:T(1024)S(1)} %fusion.6), kind=kCustom, calls=%fused_computation | custom fusion | bytes 16785408 | tf_op jit(solution)/shard_map/jit(_take)/gather | solution.py:21
  493.2 74.5 %all-gather.8.cloned.1.call-done = bf16[1024,2800]{0,1:T(8,128)(2,1)} async-done(((bf16[128,2800]{0,1:T(8,128)(2,1)}), bf16[1024,2800]{0,1:T(8,128)(2,1)}) %all-gather.8.cloned.1.call-update) | async-done | bytes 5734416 | tf_op jit(solution)/shard_map/all_gather | solution.py:23
  567.8 32.6 %convolution_bitcast_fusion = f32[2,2800,2048]{2,1,0:T(8,128)} fusion(bf16[2,1024,2048]{2,1,0:T(8,128)(2,1)} %bitcast.7, pred[2,1024]{1,0:T(4,128)(4,1)S(1)} %broadcast_in_dim.14, bf16[1024,2800]{0,1:T(8,128)(2,1)} %all-gather.8.cloned.1.call-done), kind=kOutput, calls=%fused_computation.1 | convolution fusion | flops 23492296704 | bytes 60000256 | tf_op jit(solution)/shard_map/am,oac->omc/dot_general | solution.py:24
  (3 shorter events, 0.0 us)
Async XLA Ops:
  6.5 233.3 %all-gather.4.cloned.1.call-start = ((), (), s32[]{:S(2)}) async-start(), calls=%async_computation.1 | async-start | bytes 18874368 | tf_op jit(solution)/shard_map/all_gather | solution.py:13
  7.3 402.9 %reduce-scatter.2.cloned.1.call-start = ((), (), s32[]{:S(2)}) async-start(), calls=%async_computation.2 | async-start | bytes 20971520 | tf_op jit(solution)/shard_map/reduce_scatter | solution.py:17
  285.7 128.9 %copy-start = (s32[2048]{0:T(1024)S(1)}, s32[2048]{0:T(1024)}, u32[]{:S(2)}) copy-start(s32[2048]{0:T(1024)} %param.7) | copy-start | bytes 24580
  285.7 186.7 %all-gather.6.cloned.1.call-start = ((), (), s32[]{:S(2)}) async-start(), calls=%async_computation.3 | async-start | bytes 10485760 | tf_op jit(solution)/shard_map/all_gather | solution.py:20
  414.0 153.8 %all-gather.8.cloned.1.call-start = ((), (), s32[]{:S(2)}) async-start(), calls=%async_computation.4 | async-start | bytes 6451200 | tf_op jit(solution)/shard_map/all_gather | solution.py:23
Sparse Core Ops, SparseCore 0:
  9.5 230.2 all-gather.3
  285.8 124.2 reduce-scatter.1
  414.1 58.2 all-gather.5
  474.5 93.1 all-gather.7
where the time goes:
time: 607 us
  waiting for transfers between devices  490 us (81%)
  matrix products  78.4 us (13%)
  local copies, waits for them, and re-layouts  20.8 us (3%)
  between operations  13.2 us (2%)
    all_gather x1, waiting for transfers between devices, body(): lax.all_gather(pair_block, 'rows', axis=0, tiled=True)  233 us
    reduce_scatter x1, waiting for transfers between devices, body(): lax.psum_scatter(partial_sum, 'panel', scatter_dimension=0, tiled=True)  124 us
    all_gather x1, waiting for transfers between devices, body(): coef_all = lax.all_gather(virt_coef, 'rows', axis=0, tiled=True)  74.5 us
    all_gather x1, waiting for transfers between devices, body(): gathered = lax.all_gather(own_rows, 'panel', axis=0, tiled=True)  57.8 us
    dot_general x1, matrix products, body(): jnp.dot(lax.all_gather(pair_block, 'rows', axis=0, tiled=True), resolvent...  45.8 us
    dot_general x1, matrix products, body(): jnp.einsum('am,oac->omc', coef_all, grouped, preferred_element_type=jnp.f...  32.6 us
    gather x1, local copies, waits for them, and re-layouts, body(): grouped = jnp.take(gathered, slot_row, axis=0)  20.8 us
  transfers between devices with their start and end apart: 4, of which 4 were waited for; matrix products, arithmetic and copies ran while one was open for 3% of the time, Pallas kernels for 0%

commit v1 on v0

v1 whole, which is shorter than its diff:
```python
import functools

import jax
import jax.numpy as jnp
from jax import lax
from jax.experimental import pallas as pl
from jax.experimental.pallas import tpu as pltpu
from jax.sharding import PartitionSpec as P

OCC_B = 2
LAGS = (None, None, 1, None)
VMEM_LIMIT = 56 * 1024 * 1024
BF16, F32 = jnp.bfloat16, jnp.float32


def divisor_tile(size, step, top):
    best = [t for t in range(step, min(size, top) + 1, step) if size % t == 0]
    return best[-1] if best else size


def bit_reversed(n):
    order = [0]
    while len(order) < n:
        order = [2 * j for j in order] + [2 * j + 1 for j in order]
    return order


def params():
    return pltpu.CompilerParams(
        dimension_semantics=("arbitrary",), vmem_limit_bytes=VMEM_LIMIT
    )


def split_store(res, keep_ref, send_ref, place, order):
    part = res.shape[0] // len(order)
    half = max(len(order) // 2, 1)
    for slot, j in enumerate(order):
        rows = res[pl.ds(pl.multiple_of((place ^ j) * part, part), part), :]
        if slot < half:
            keep_ref[slot * part : (slot + 1) * part, :] = rows
        else:
            send_ref[(slot - half) * part : (slot - half + 1) * part, :] = rows


def first_kernel(order, place_ref, lhs_ref, r_ref, r16_ref, keep_ref, send_ref, res):
    r16_ref[...] = r_ref[...].astype(BF16)
    res[...] = jnp.dot(lhs_ref[...], r16_ref[...], preferred_element_type=F32)
    split_store(res, keep_ref, send_ref, place_ref[0], order)


def first_product(place, lhs, resolvent, order):
    rows, depth = lhs.shape
    cols = resolvent.shape[1]
    tile = divisor_tile(cols, 128, 256)
    half = rows // 2
    return pl.pallas_call(
        functools.partial(first_kernel, order),
        grid_spec=pltpu.PrefetchScalarGridSpec(
            num_scalar_prefetch=1,
            grid=(cols // tile,),
            in_specs=[
                pl.BlockSpec((rows, depth), lambda i, s: (0, 0)),
                pl.BlockSpec((depth, tile), lambda i, s: (0, i)),
            ],
            out_specs=[
                pl.BlockSpec((depth, tile), lambda i, s: (0, i)),
                pl.BlockSpec((half, tile), lambda i, s: (0, i)),
                pl.BlockSpec((half, tile), lambda i, s: (0, i)),
            ],
            scratch_shapes=[pltpu.VMEM((rows, tile), F32)],
        ),
        out_shape=[
            jax.ShapeDtypeStruct((depth, cols), BF16),
            jax.ShapeDtypeStruct((half, cols), F32),
            jax.ShapeDtypeStruct((half, cols), F32),
        ],
        compiler_params=params(),
        cost_estimate=pl.CostEstimate(
            flops=0, bytes_accessed=0, transcendentals=0
        ),
        name="first_product",
    )(place, lhs, resolvent)


def group_kernel(n, order, place_ref, *refs):
    pieces, (r_ref, keep_ref, send_ref, lhs, res) = refs[:n], refs[n:]

    @pl.when(pl.program_id(0) == 0)
    def _():
        at = 0
        for piece in pieces:
            lhs[at : at + piece.shape[0], :] = piece[...]
            at += piece.shape[0]

    res[...] = jnp.dot(lhs[...], r_ref[...], preferred_element_type=F32)
    split_store(res, keep_ref, send_ref, place_ref[0], order)


def group_product(place, pieces, r16, order):
    rows = sum(piece.shape[0] for piece in pieces)
    depth, cols = r16.shape
    tile = divisor_tile(cols, 128, 512)
    half = rows // 2
    return pl.pallas_call(
        functools.partial(group_kernel, len(pieces), order),
        grid_spec=pltpu.PrefetchScalarGridSpec(
            num_scalar_prefetch=1,
            grid=(cols // tile,),
            in_specs=[pl.BlockSpec(piece.shape, lambda i, s: (0, 0)) for piece in pieces]
            + [pl.BlockSpec((depth, tile), lambda i, s: (0, i))],
            out_specs=[
                pl.BlockSpec((half, tile), lambda i, s: (0, i)),
                pl.BlockSpec((half, tile), lambda i, s: (0, i)),
            ],
            scratch_shapes=[pltpu.VMEM((rows, depth), BF16), pltpu.VMEM((rows, tile), F32)],
        ),
        out_shape=[jax.ShapeDtypeStruct((half, cols), F32)] * 2,
        compiler_params=params(),
        cost_estimate=pl.CostEstimate(
            flops=0, bytes_accessed=0, transcendentals=0
        ),
        name="group_product",
    )(place, *pieces, r16)


def back_kernel(n, m, *refs):
    coefs, refs = refs[:n], refs[n:]
    if m:
        slots_ref, ids, gammas, refs = refs[0], refs[1 : 1 + m], refs[1 + m : 1 + 2 * m], refs[1 + 2 * m :]
        g_ref, out_ref, whole_ref, lhs, picks = refs
    else:
        g_ref, _, out_ref, lhs = refs
        whole_ref = g_ref
    occ, depth, tile = g_ref.shape

    @pl.when(pl.program_id(0) == 0)
    def _():
        at = 0
        for c in coefs:
            lhs[:, at : at + c.shape[1]] = c[...]
            at += c.shape[1]
        at = 0
        for i in range(m):
            wide = ids[i].shape[1]
            picks[:, at : at + wide] = (slots_ref[...] == ids[i][...]).astype(F32).astype(BF16)
            at += wide

    for o in range(occ):
        if m:
            placed = g_ref[o].astype(F32)
            at = 0
            for i in range(m):
                wide = ids[i].shape[1]
                placed += jnp.dot(
                    picks[o * depth : (o + 1) * depth, at : at + wide],
                    gammas[i][...],
                    preferred_element_type=F32,
                )
                at += wide
            whole_ref[o] = placed.astype(BF16)
        out_ref[o] = jnp.dot(lhs[...], whole_ref[o], preferred_element_type=F32)


def back_product(coefs, late, grouped, total, first, out):
    chunk = coefs[0].shape[0]
    occ, depth, cols = grouped.shape
    tile = divisor_tile(cols, 128, 256)
    n, m = len(coefs), 0
    at_col = lambda i: (0, 0, i)
    specs = [pl.BlockSpec(c.shape, lambda i: (0, 0)) for c in coefs]
    whole = (pl.Element(occ), pl.Element(chunk), pl.Element(tile))
    out_specs = [pl.BlockSpec(whole, lambda i: (0, first, i * tile))]
    shapes = [jax.ShapeDtypeStruct((occ, total, cols), F32)]
    scratch = [pltpu.VMEM((chunk, depth), BF16)]
    args = list(coefs)
    aliases = {}
    if late is not None:
        slots, ids, gammas = late
        m = len(ids)
        args += [slots, *ids, *gammas, grouped]
        specs += [pl.BlockSpec(slots.shape, lambda i: (0, 0))]
        specs += [pl.BlockSpec(v.shape, lambda i: (0, 0)) for v in ids]
        specs += [pl.BlockSpec((g.shape[0], tile), lambda i: (0, i)) for g in gammas]
        specs += [pl.BlockSpec((occ, depth, tile), at_col)]
        out_specs.append(pl.BlockSpec((occ, depth, tile), at_col))
        shapes.append(jax.ShapeDtypeStruct(grouped.shape, BF16))
        scratch.append(pltpu.VMEM((occ * depth, sum(v.shape[1] for v in ids)), BF16))
    else:
        args += [grouped, out]
        specs += [pl.BlockSpec((occ, depth, tile), at_col), pl.BlockSpec(memory_space=pl.ANY)]
        aliases = {len(args) - 1: 0}
    return pl.pallas_call(
        functools.partial(back_kernel, n, m),
        grid=(cols // tile,),
        in_specs=specs,
        out_specs=out_specs,
        out_shape=shapes,
        scratch_shapes=scratch,
        input_output_aliases=aliases,
        compiler_params=params(),
        cost_estimate=pl.CostEstimate(
            flops=0, bytes_accessed=0, transcendentals=0
        ),
        name="back_product",
    )(*args)


def tied(value, *after):
    return lax.optimization_barrier((value, *after))[0]


def body(rows, panel, pair_block, resolvent, virt_coef, slot_row):
    high = rows // 2
    up = [(r, (r + 2) % rows) for r in range(rows)]
    down = [(r, (r - 2) % rows) for r in range(rows)]
    swap = [(r, r ^ 1) for r in range(rows)]
    me_row, me_panel = lax.axis_index("rows"), lax.axis_index("panel")
    order = bit_reversed(panel)
    place = me_panel.astype(jnp.int32).reshape(1)
    stages = [1 << k for k in range((panel - 1).bit_length())]

    def over_rows(v, pairs):
        return lax.ppermute(v, "rows", pairs)

    def over_panel(v, width):
        return lax.ppermute(v, "panel", [(q, q ^ width) for q in range(panel)])

    def block_of(s, cross):
        return (me_row // 2 + (high - s)) % high * 2 + ((me_row % 2) ^ cross)

    def spread(pieces, fence):
        straight = [dict(enumerate(pieces))]
        crossed = []
        arrivals = []
        for s in range(high - 1):
            straight.append({})
            crossed.append({})
            for c in range(2):
                got = [over_rows(straight[s][c], up), over_rows(straight[s][c], swap)]
                straight[s + 1][c], crossed[s][c] = got = fence(got)
                arrivals.append([((s + 1, 0, c), got[0]), ((s, 1, c), got[1])])
        s = high - 1
        ends = [over_rows(straight[s][0], swap)]
        if high > 1:
            ends.append(over_rows(tied(crossed[0][1], straight[s][0]), down))
        else:
            ends.append(over_rows(straight[s][1], swap))
        ends = fence(ends)
        arrivals.append([((s, 1, c), ends[c]) for c in range(2)])
        return arrivals

    vblock = virt_coef.shape[0]
    sequence = [(0, 0)] + [
        key for s in range(high) for key in ([(s + 1, 0)] if s < high - 1 else []) + [(s, 1)]
    ]
    by_block = slot_row.reshape(OCC_B, rows, vblock)
    slots = jnp.concatenate(
        [lax.dynamic_slice_in_dim(by_block, block_of(*key), 1, axis=1) for key in sequence], axis=1
    ).reshape(-1, 1)

    size = pair_block.shape[0]
    step = size // 2

    def row_ids(keys):
        natural = jnp.concatenate(
            [block_of(s, x) * size + c * step + jnp.arange(step, dtype=jnp.int32) for s, x, c in keys]
        )
        cut_ids = natural.reshape(panel, -1)
        return jnp.concatenate([cut_ids[me_panel ^ j] for j in order]).reshape(1, -1)

    parts, sums, owns, gammas, ids = [], [], [], [], []

    def panel_sum(keep, send, keys):
        parts.append(send)
        for k, width in enumerate(stages):
            got = over_panel(send, width)
            if k + 1 < len(stages):
                half = keep.shape[0] // 2
                send = keep[half:] + got[half:]
                keep = (keep[:half], got[:half])
                sums.append(send) if k == 0 else None
                keep = keep[0] + keep[1]
            else:
                keep = keep + got
        own = keep.astype(BF16)
        owns.append(own)
        for width in reversed(stages):
            own = jnp.concatenate([own, over_panel(own, width)], axis=0)
        gammas.append(own)
        ids.append(row_ids(keys))

    def regroup(grouped, which):
        gamma = jnp.concatenate([gammas[k] for k in which], axis=0)
        pick = (slots == jnp.concatenate([ids[k] for k in which], axis=1)).astype(BF16)
        placed = jnp.dot(pick, gamma, preferred_element_type=F32)
        if grouped is not None:
            placed = placed + grouped.astype(F32)
        return placed.astype(BF16)

    piece0 = pair_block[:step]
    piece1 = tied(pair_block, piece0)[step:]
    r16, keep, send = first_product(place, pair_block, resolvent, order)
    panel_sum(keep, send, [(0, 0, 0), (0, 0, 1)])
    grouped = None
    count = 2 * (high - 1) + 1
    batch = max(1, 512 // (2 * step))
    closing = [len(range(0, h + 1)) for h in range(count)]
    closes = {h for h in range(count) if h >= count - 3 or (h + 1) % batch == 0 or h == count - 4}
    pending = []
    marks = []

    def fence(got):
        h = len(marks)
        after = []
        if h:
            for kind, lag in zip((parts, sums, owns, gammas), LAGS):
                if lag is not None and len(kind) > lag:
                    after.append(kind[-1 - lag])
        got = list(lax.optimization_barrier((*got, *after)))[: len(got)]
        marks.append(got[0])
        return got

    coef_at = max(count - 2, 0)
    arrivals = None

    state = {"grouped": None}

    def take(h, items):
        pending.extend(items)
        if h not in closes:
            return
        keep, send = group_product(place, [v for _, v in pending], r16, order)
        panel_sum(keep, send, [key for key, _ in pending])
        pending.clear()
        k = len(gammas) - 1
        if k >= 3 and k % 2:
            state["grouped"] = regroup(state["grouped"], [k - 3, k - 2])

    straight = [{0: piece0, 1: piece1}]
    crossed = []
    h = 0
    for s in range(high - 1):
        straight.append({})
        crossed.append({})
        for c in range(2):
            got = fence([over_rows(straight[s][c], up), over_rows(straight[s][c], swap)])
            straight[s + 1][c], crossed[s][c] = got
            take(h, [((s + 1, 0, c), got[0]), ((s, 1, c), got[1])])
            h += 1
    s = high - 1
    ends = [over_rows(straight[s][0], swap)]
    if high > 1:
        ends.append(over_rows(tied(crossed[0][1], straight[s][0]), down))
    else:
        ends.append(over_rows(straight[s][1], swap))
    ends = fence(ends)
    take(h, [((s, 1, c), ends[c]) for c in range(2)])

    done = len(gammas) - 2 if len(gammas) % 2 == 0 else len(gammas) - 1
    late = list(range(0 if state["grouped"] is None else done, len(gammas)))
    grouped = state["grouped"]
    if grouped is None:
        grouped = jnp.zeros((slots.shape[0], gammas[0].shape[1]), BF16)

    coef = tied(virt_coef, marks[max(len(marks) - 2, 0)]).T
    total = coef.shape[0]
    cut = divisor_tile(total, 16, total // 2)
    cut = total // 16 // 2 * 16
    arrived = [{}, {}]
    for items in spread([coef[:cut], coef[cut:]], lambda got: got):
        for (back, x, c), v in items:
            arrived[c][(back, x)] = v
    arrived[0][(0, 0)], arrived[1][(0, 0)] = coef[:cut], coef[cut:]
    grouped = grouped.reshape(OCC_B, rows * vblock, -1)
    out = None
    for c, first in enumerate((0, cut)):
        parts = [arrived[c][key] for key in sequence]
        if vblock % 128:
            parts = [jnp.concatenate(parts, axis=1)]
        if c == 0:
            out, grouped = back_product(
                parts, (slots, [ids[k] for k in late], [gammas[k] for k in late]), grouped, total, first, None
            )
        else:
            (out,) = back_product(parts, None, grouped, total, first, out)
    return out


def solution(mesh):
    placed = (P("rows", "panel"), P("panel", "rows"), P("rows", "panel"), P())
    return jax.shard_map(
        functools.partial(body, mesh.shape["rows"], mesh.shape["panel"]),
        mesh=mesh,
        in_specs=placed,
        out_specs=P(None, "panel", "rows"),
        check_vma=False,
    )
```

time: 607 us -> 377 us (0.62)
  waiting for transfers between devices: 490 us -> 149 us
  Pallas kernels: 0 us -> 125 us
  matrix products: 78.4 us -> 16.6 us
  starting transfers between devices: 0.3 us -> 45.2 us
  other arithmetic: 3.84 us -> 20.1 us
  between operations: 13.2 us -> 0.64 us
    all_gather x3 -> x0, waiting for transfers between devices: 365 us -> none  [the longest x1 233 us: body(): lax.all_gather(pair_block, 'rows', axis=0, tiled=True)]
    ppermute x0 -> x52, waiting for transfers between devices: none -> 149 us  [the longest x28 93.6 us: over_rows(): return lax.ppermute(v, 'rows', pairs)]
    pallas_call x0 -> x8, Pallas kernels: none -> 125 us  [the longest x5 60.7 us: group_product(): pl.pallas_call(functools.partial(group_kernel, len(pieces), order), grid_...]
    reduce_scatter x1 -> x0, waiting for transfers between devices: 124 us -> none  [body(): lax.psum_scatter(partial_sum, 'panel', scatter_dimension=0, tiled=True)]
    dot_general x2, matrix products: 78.4 us -> 16.6 us  [regroup(): placed = jnp.dot(pick, gamma, preferred_element_type=F32)]
    ppermute x0 -> x52, starting transfers between devices: none -> 45.2 us  [the longest x28 29.2 us: over_rows(): return lax.ppermute(v, 'rows', pairs)]
    gather x1 -> x0, local copies, waits for them, and re-layouts: 20.8 us -> none  [body(): grouped = jnp.take(gathered, slot_row, axis=0)]
    unnamed x2 -> x76, local copies, waits for them, and re-layouts: 0.01 us -> 10.7 us
  transfers between devices with their start and end apart: 4 -> 52, of which waited for: 4 -> 16; matrix products, arithmetic and copies ran while one was open for 3% -> 13% of each run, Pallas kernels for 0% -> 23%
where the time goes in v1:
time: 377 us; the launch traced here: 376 us
  waiting for transfers between devices  149 us (40%)
  Pallas kernels  125 us (33%)
  starting transfers between devices  45.2 us (12%)
  other arithmetic  20.1 us (5%)
  local copies, waits for them, and re-layouts  18.8 us (5%)
  matrix products  16.6 us (4%)
    ppermute x28, waiting for transfers between devices, over_rows(): return lax.ppermute(v, 'rows', pairs)  93.6 us
    pallas_call x5, Pallas kernels, group_product(): pl.pallas_call(functools.partial(group_kernel, len(pieces), order), grid_...  60.7 us
    ppermute x24, waiting for transfers between devices, over_panel(): return lax.ppermute(v, 'panel', [(q, q ^ width) for q in range(panel)])  55.2 us
    pallas_call x2, Pallas kernels, back_product(): pl.pallas_call(functools.partial(back_kernel, n, m), grid=(cols // tile,)...  44.6 us
    ppermute x28, starting transfers between devices, over_rows(): return lax.ppermute(v, 'rows', pairs)  29.2 us
    pallas_call x1, Pallas kernels, first_product(): pl.pallas_call(functools.partial(first_kernel, order), grid_spec=pltpu.Pr...  20.2 us
    dot_general x2, matrix products, regroup(): placed = jnp.dot(pick, gamma, preferred_element_type=F32)  16.6 us
    ppermute x24, starting transfers between devices, over_panel(): return lax.ppermute(v, 'panel', [(q, q ^ width) for q in range(panel)])  16 us
  transfers between devices with their start and end apart: 52, of which 16 were waited for; matrix products, arithmetic and copies ran while one was open for 13% of the time, Pallas kernels for 23%

profile of v1, /device:TPU:0, one launch (start us, length us, event | category | flops | bytes accessed | tf_op | source)
XLA Modules:
  0.0 375.6 jit_solution(16808248018058596113)
XLA Ops:
  0.0 20.2 %first_product.1 = (bf16[4096,2048]{1,0:T(8,128)(2,1)}, f32[128,2048]{1,0:T(8,128)}, f32[128,2048]{1,0:T(8,128)}) custom-call(s32[1]{0:T(128)} %bitcast.place_ref, bf16[256,4096]{1,0:T(8,128)(2,1)} %lhs_ref.1, f32[4096,2048]{1,0:T(8,128)} %r_ref.1), custom_call_target="tpu_custom_call" | custom-call | tf_op jit(solution)/shard_map/first_product/pallas_call | solution.py:56
  22.3 2.4 collective-permute-start.1
  31.3 17.6 %collective-permute-done.1.refs_3_ = bf16[128,4096]{1,0:T(8,128)(2,1)S(1)} collective-permute-done((bf16[128,4096]{1,0:T(8,128)(2,1)}, bf16[128,4096]{1,0:T(8,128)(2,1)S(1)}, u32[]{:S(2)}, u32[]{:S(2)}) %collective-permute-start.1) | collective-permute-done | bytes 1048608 | tf_op jit(solution)/shard_map/ppermute | solution.py:223
  49.0 3.8 %collective-permute-done.refs_2_ = bf16[128,4096]{1,0:T(8,128)(2,1)S(1)} collective-permute-done((bf16[128,4096]{1,0:T(8,128)(2,1)}, bf16[128,4096]{1,0:T(8,128)(2,1)S(1)}, u32[]{:S(2)}, u32[]{:S(2)}) %collective-permute-start) | collective-permute-done | bytes 1048608 | tf_op jit(solution)/shard_map/ppermute | solution.py:223
  53.0 18.4 %collective-permute-done.9.refs_1_ = bf16[128,4096]{1,0:T(8,128)(2,1)S(1)} collective-permute-done((bf16[128,4096]{1,0:T(8,128)(2,1)}, bf16[128,4096]{1,0:T(8,128)(2,1)S(1)}, u32[]{:S(2)}, u32[]{:S(2)}) %collective-permute-start.9) | collective-permute-done | bytes 1048608 | tf_op jit(solution)/shard_map/ppermute | solution.py:223
  71.4 3.9 %collective-permute-done.8.refs_0_ = bf16[128,4096]{1,0:T(8,128)(2,1)} collective-permute-done((bf16[128,4096]{1,0:T(8,128)(2,1)}, bf16[128,4096]{1,0:T(8,128)(2,1)}, u32[]{:S(2)}, u32[]{:S(2)}) %collective-permute-start.8) | collective-permute-done | bytes 1048608 | tf_op jit(solution)/shard_map/ppermute | solution.py:223
  75.7 14.7 %group_product.7 = (f32[256,2048]{1,0:T(8,128)}, f32[256,2048]{1,0:T(8,128)}) custom-call(s32[1]{0:T(128)} %bitcast.place_ref, bf16[128,4096]{1,0:T(8,128)(2,1)} %collective-permute-done.8.refs_0_, bf16[128,4096]{1,0:T(8,128)(2,1)} %copy-done.9, bf16[128,4096]{1,0:T(8,128)(2,1)} %copy-done.8, bf16[128,4096]{1,0:T(8,128)(2,1)} %copy-done.7, ...), custom_call_target="tpu_custom_call" | custom-call | tf_op jit(solution)/shard_map/group_product/pallas_call | solution.py:104
  91.2 2.1 constant_dynamic-update-slice_fusion.11
  93.3 23.0 %collective-permute-done.11.refs_1_ = bf16[128,4096]{1,0:T(8,128)(2,1)} collective-permute-done((bf16[128,4096]{1,0:T(8,128)(2,1)}, bf16[128,4096]{1,0:T(8,128)(2,1)}, u32[]{:S(2)}, u32[]{:S(2)}) %collective-permute-start.11) | collective-permute-done | bytes 1048608 | tf_op jit(solution)/shard_map/ppermute | solution.py:223
  116.3 3.4 collective-permute-done.10.refs_0_
  119.6 14.6 %group_product.5 = (f32[256,2048]{1,0:T(8,128)}, f32[256,2048]{1,0:T(8,128)}) custom-call(s32[1]{0:T(128)} %bitcast.place_ref, bf16[128,4096]{1,0:T(8,128)(2,1)} %collective-permute-done.10.refs_0_, bf16[128,4096]{1,0:T(8,128)(2,1)} %collective-permute-done.11.refs_1_, bf16[128,4096]{1,0:T(8,128)(2,1)} %collective-permute-done.2.refs_2_, ...), custom_call_target="tpu_custom_call" | custom-call | tf_op jit(solution)/shard_map/group_product/pallas_call | solution.py:104
  136.1 7.1 %collective-permute-done.48 = bf16[64,2048]{1,0:T(8,128)(2,1)S(1)} collective-permute-done((bf16[64,2048]{1,0:T(8,128)(2,1)S(1)}, bf16[64,2048]{1,0:T(8,128)(2,1)S(1)}, u32[]{:S(2)}, u32[]{:S(2)}) %collective-permute-start.48) | collective-permute-done | bytes 262176 | tf_op jit(solution)/shard_map/ppermute | solution.py:226
  152.3 17.8 %collective-permute-done.35 = f32[128,2048]{1,0:T(8,128)S(1)} collective-permute-done((f32[128,2048]{1,0:T(8,128)S(1)}, f32[128,2048]{1,0:T(8,128)S(1)}, u32[]{:S(2)}, u32[]{:S(2)}) %collective-permute-start.35) | collective-permute-done | bytes 1048608 | tf_op jit(solution)/shard_map/ppermute | solution.py:226
  175.0 10.4 %group_product.8 = (f32[128,2048]{1,0:T(8,128)}, f32[128,2048]{1,0:T(8,128)}) custom-call(s32[1]{0:T(128)} %bitcast.place_ref, bf16[128,4096]{1,0:T(8,128)(2,1)} %collective-permute-done.32.refs_0_, bf16[128,4096]{1,0:T(8,128)(2,1)} %copy-done.17, bf16[4096,2048]{1,0:T(8,128)(2,1)} %get-tuple-element.47.refs_4_.refs_2_), custom_call_target="tpu_custom_call" | custom-call | tf_op jit(solution)/shard_map/group_product/pallas_call | solution.py:104
  185.4 7.3 %collective-permute-done.13 = f32[128,2048]{1,0:T(8,128)} collective-permute-done((f32[128,2048]{1,0:T(8,128)}, f32[128,2048]{1,0:T(8,128)}, u32[]{:S(2)}, u32[]{:S(2)}) %collective-permute-start.13) | collective-permute-done | bytes 1048608 | tf_op jit(solution)/shard_map/ppermute | solution.py:226
  192.7 2.2 constant_dynamic-update-slice_fusion.5
  197.1 1.6 collective-permute-start.36
  198.6 3.9 %collective-permute-start.37 = (bf16[128,4096]{1,0:T(8,128)(2,1)}, bf16[128,4096]{1,0:T(8,128)(2,1)S(1)}, u32[]{:S(2)}, u32[]{:S(2)}) collective-permute-start(bf16[128,4096]{1,0:T(8,128)(2,1)} %copy-done.7), channel_id=1, source_target_pairs={{0,24},{4,28},{8,0},{12,4},{16,8},{20,12},{24,16},{28,20},{1,25},{... | collective-permute-start | bytes 3145736 | tf_op jit(solution)/shard_map/ppermute | solution.py:223
  202.5 10.6 %group_product.6 = (f32[128,2048]{1,0:T(8,128)}, f32[128,2048]{1,0:T(8,128)}) custom-call(s32[1]{0:T(128)} %bitcast.place_ref, bf16[128,4096]{1,0:T(8,128)(2,1)} %collective-permute-done.6.refs_0_, bf16[128,4096]{1,0:T(8,128)(2,1)} %collective-permute-done.7.refs_1_, bf16[4096,2048]{1,0:T(8,128)(2,1)} %get-tuple-element.47.refs_4_.refs_2_), custom_call_target="tpu_custom_call" | custom-call | tf_op jit(solution)/shard_map/group_product/pallas_call | solution.py:104
  221.3 11.0 %collective-permute-done.39 = f32[64,2048]{1,0:T(8,128)S(1)} collective-permute-done((f32[64,2048]{1,0:T(8,128)S(1)}, f32[64,2048]{1,0:T(8,128)S(1)}, u32[]{:S(2)}, u32[]{:S(2)}) %collective-permute-start.39) | collective-permute-done | bytes 524320 | tf_op jit(solution)/shard_map/ppermute | solution.py:226
  232.8 1.8 constant_dynamic-update-slice_fusion.2
  236.0 10.4 %group_product.9 = (f32[128,2048]{1,0:T(8,128)}, f32[128,2048]{1,0:T(8,128)}) custom-call(s32[1]{0:T(128)} %bitcast.place_ref, bf16[128,4096]{1,0:T(8,128)(2,1)} %copy-done.15, bf16[128,4096]{1,0:T(8,128)(2,1)} %copy-done.16, bf16[4096,2048]{1,0:T(8,128)(2,1)} %get-tuple-element.47.refs_4_.refs_2_), custom_call_target="tpu_custom_call" | custom-call | tf_op jit(solution)/shard_map/group_product/pallas_call | solution.py:104
  253.5 2.3 constant_dynamic-update-slice_fusion.6
  255.8 5.5 %collective-permute-done.21.refs_3_ = bf16[1392,128]{1,0:T(8,128)(2,1)S(1)} collective-permute-done((bf16[1392,128]{1,0:T(8,128)(2,1)}, bf16[1392,128]{1,0:T(8,128)(2,1)S(1)}, u32[]{:S(2)}, u32[]{:S(2)}) %collective-permute-start.21) | collective-permute-done | bytes 356384 | tf_op jit(solution)/shard_map/ppermute | solution.py:223
  267.3 7.6 %fusion = bf16[2048,2048]{1,0:T(8,128)(2,1)S(1)} fusion(bf16[768,2048]{1,0:T(8,128)(2,1)S(1)} %copy-done.33, s32[768]{0:T(1024)S(1)} %add_reduce_fusion.1, s32[2048]{0:T(1024)S(1)} %bitcast.70), kind=kOutput, calls=%fused_computation.1 | convolution fusion | flops 6444023808 | bytes 11545600 | tf_op jit(solution)/shard_map/dot_general | solution.py:295
  278.5 7.3 %collective-permute-done.41 = f32[64,2048]{1,0:T(8,128)S(1)} collective-permute-done((f32[64,2048]{1,0:T(8,128)S(1)}, f32[64,2048]{1,0:T(8,128)S(1)}, u32[]{:S(2)}, u32[]{:S(2)}) %collective-permute-start.41) | collective-permute-done | bytes 524320 | tf_op jit(solution)/shard_map/ppermute | solution.py:226
  289.2 4.5 %collective-permute-done.42 = bf16[64,2048]{1,0:T(8,128)(2,1)S(1)} collective-permute-done((bf16[64,2048]{1,0:T(8,128)(2,1)S(1)}, bf16[64,2048]{1,0:T(8,128)(2,1)S(1)}, u32[]{:S(2)}, u32[]{:S(2)}) %collective-permute-start.42) | collective-permute-done | bytes 262176 | tf_op jit(solution)/shard_map/ppermute | solution.py:226
  294.3 9.0 %add_convert_fusion = bf16[2048,2048]{1,0:T(8,128)(2,1)} fusion(bf16[2048,2048]{1,0:T(8,128)(2,1)S(1)} %fusion, bf16[768,2048]{1,0:T(8,128)(2,1)S(1)} %constant_dynamic-update-slice_fusion, s32[768]{0:T(1024)S(1)} %add_reduce_fusion, s32[2048]{0:T(1024)S(1)} %bitcast.71), kind=kOutput, calls=%fused_computation | convolution fusion | flops 6456606720 | bytes 19934208 | tf_op jit(solution)/shard_map/dot_general | solution.py:295
  305.4 3.8 %collective-permute-start.23 = (bf16[1408,128]{1,0:T(8,128)(2,1)S(1)}, bf16[1408,128]{1,0:T(8,128)(2,1)S(1)}, u32[]{:S(2)}, u32[]{:S(2)}) collective-permute-start(bf16[1408,128]{1,0:T(8,128)(2,1)S(1)} %collective-permute-done.15.refs_2_), channel_id=1, source_target_pairs={{0,24},{4,28},{8,0},{12,4},{16,8},{20,12},{24,16},{28,20},{1,25},{... | collective-permute-start | bytes 1081352 | tf_op jit(solution)/shard_map/ppermute | solution.py:223
  312.3 16.8 %collective-permute-done.27.refs_7_ = bf16[1392,128]{1,0:T(8,128)(2,1)S(1)} collective-permute-done((bf16[1392,128]{1,0:T(8,128)(2,1)S(1)}, bf16[1392,128]{1,0:T(8,128)(2,1)S(1)}, u32[]{:S(2)}, u32[]{:S(2)}) %collective-permute-start.27) | collective-permute-done | bytes 356384 | tf_op jit(solution)/shard_map/ppermute | solution.py:223
  329.9 25.2 %back_product.2 = (f32[2,2800,2048]{2,1,0:T(8,128)}, bf16[2,1024,2048]{2,1,0:T(8,128)(2,1)}) custom-call(bf16[1392,128]{1,0:T(8,128)(2,1)} %copy-done.6, bf16[1392,128]{1,0:T(8,128)(2,1)} %collective-permute-done.20.refs_1_, bf16[1392,128]{1,0:T(8,128)(2,1)} %copy-done.28, bf16[1392,128]{1,0:T(8,128)(2,1)} %copy-done.26, bf16[1392,128]{1,0:T(8,128)(2,1)} %copy-done.29, ...), custom_call_target="tpu_custom_call" | custom-call | tf_op jit(solution)/shard_map/back_product/pallas_call | solution.py:192
  356.3 19.3 %back_product.3 = f32[2,2800,2048]{2,1,0:T(8,128)} custom-call(bf16[1408,128]{1,0:T(8,128)(2,1)} %copy-done.5, bf16[1408,128]{1,0:T(8,128)(2,1)} %copy-done.20, bf16[1408,128]{1,0:T(8,128)(2,1)} %copy-done.19, bf16[1408,128]{1,0:T(8,128)(2,1)} %copy-done.21, bf16[1408,128]{1,0:T(8,128)(2,1)} %copy-done.22, ...), custom_call_target="tpu_custom_call", output_to_operand_aliasing={{}: (9, {})} | custom-call | tf_op jit(solution)/shard_map/back_product/pallas_call | solution.py:192
  (220 shorter events, 65.6 us)
Async XLA Ops:
  22.3 26.6 %collective-permute-start.1 = (bf16[128,4096]{1,0:T(8,128)(2,1)}, bf16[128,4096]{1,0:T(8,128)(2,1)S(1)}, u32[]{:S(2)}, u32[]{:S(2)}) collective-permute-start(bf16[128,4096]{1,0:T(8,128)(2,1)} %slice.87), channel_id=1, source_target_pairs={{0,4},{4,0},{8,12},{12,8},{16,20},{20,16},{24,28},{28,24},{1,5},{5... | collective-permute-start | bytes 3145736 | tf_op jit(solution)/shard_map/ppermute | solution.py:223
  24.7 28.0 %collective-permute-start = (bf16[128,4096]{1,0:T(8,128)(2,1)}, bf16[128,4096]{1,0:T(8,128)(2,1)S(1)}, u32[]{:S(2)}, u32[]{:S(2)}) collective-permute-start(bf16[128,4096]{1,0:T(8,128)(2,1)} %slice.87), channel_id=1, source_target_pairs={{0,8},{4,12},{8,16},{12,20},{16,24},{20,28},{24,0},{28,4},{1,9},{5... | collective-permute-start | bytes 3145736 | tf_op jit(solution)/shard_map/ppermute | solution.py:223
  26.3 45.1 %collective-permute-start.9 = (bf16[128,4096]{1,0:T(8,128)(2,1)}, bf16[128,4096]{1,0:T(8,128)(2,1)S(1)}, u32[]{:S(2)}, u32[]{:S(2)}) collective-permute-start(bf16[128,4096]{1,0:T(8,128)(2,1)} %slice.86), channel_id=1, source_target_pairs={{0,4},{4,0},{8,12},{12,8},{16,20},{20,16},{24,28},{28,24},{1,5},{5... | collective-permute-start | bytes 3145736 | tf_op jit(solution)/shard_map/ppermute | solution.py:223
  26.8 48.5 %collective-permute-start.8 = (bf16[128,4096]{1,0:T(8,128)(2,1)}, bf16[128,4096]{1,0:T(8,128)(2,1)}, u32[]{:S(2)}, u32[]{:S(2)}) collective-permute-start(bf16[128,4096]{1,0:T(8,128)(2,1)} %slice.86), channel_id=1, source_target_pairs={{0,8},{4,12},{8,16},{12,20},{16,24},{20,28},{24,0},{28,4},{1,9},{5... | collective-permute-start | bytes 3145736 | tf_op jit(solution)/shard_map/ppermute | solution.py:223
  29.8 60.6 %collective-permute-start.5 = (f32[64,2048]{1,0:T(8,128)S(1)}, f32[64,2048]{1,0:T(8,128)S(1)}, u32[]{:S(2)}, u32[]{:S(2)}) collective-permute-start(f32[64,2048]{1,0:T(8,128)S(1)} %slice_add_fusion.10), channel_id=1, source_target_pairs={{0,2},{1,3},{2,0},{3,1},{4,6},{5,7},{6,4},{7,5},{8,10},{9,11},{10,... | collective-permute-start | bytes 1572872 | tf_op jit(solution)/shard_map/ppermute | solution.py:226
  52.7 66.9 %collective-permute-start.3 = (bf16[128,4096]{1,0:T(8,128)(2,1)S(1)}, bf16[128,4096]{1,0:T(8,128)(2,1)}, u32[]{:S(2)}, u32[]{:S(2)}) collective-permute-start(bf16[128,4096]{1,0:T(8,128)(2,1)S(1)} %collective-permute-done.refs_2_), channel_id=1, source_target_pairs={{0,4},{4,0},{8,12},{12,8},{16,20},{20,16},{24,28},{28,24},{1,5},{5... | collective-permute-start | bytes 3145736 | tf_op jit(solution)/shard_map/ppermute | solution.py:223
  53.0 66.6 %collective-permute-start.2 = (bf16[128,4096]{1,0:T(8,128)(2,1)S(1)}, bf16[128,4096]{1,0:T(8,128)(2,1)}, u32[]{:S(2)}, u32[]{:S(2)}) collective-permute-start(bf16[128,4096]{1,0:T(8,128)(2,1)S(1)} %collective-permute-done.refs_2_), channel_id=1, source_target_pairs={{0,8},{4,12},{8,16},{12,20},{16,24},{20,28},{24,0},{28,4},{1,9},{5... | collective-permute-start | bytes 3145736 | tf_op jit(solution)/shard_map/ppermute | solution.py:223
  75.3 41.0 %collective-permute-start.11 = (bf16[128,4096]{1,0:T(8,128)(2,1)}, bf16[128,4096]{1,0:T(8,128)(2,1)}, u32[]{:S(2)}, u32[]{:S(2)}) collective-permute-start(bf16[128,4096]{1,0:T(8,128)(2,1)} %collective-permute-done.8.refs_0_), channel_id=1, source_target_pairs={{0,4},{4,0},{8,12},{12,8},{16,20},{20,16},{24,28},{28,24},{1,5},{5... | collective-permute-start | bytes 3145736 | tf_op jit(solution)/shard_map/ppermute | solution.py:223
  75.6 44.0 %collective-permute-start.10 = (bf16[128,4096]{1,0:T(8,128)(2,1)}, bf16[128,4096]{1,0:T(8,128)(2,1)}, u32[]{:S(2)}, u32[]{:S(2)}) collective-permute-start(bf16[128,4096]{1,0:T(8,128)(2,1)} %collective-permute-done.8.refs_0_), channel_id=1, source_target_pairs={{0,8},{4,12},{8,16},{12,20},{16,24},{20,28},{24,0},{28,4},{1,9},{5... | collective-permute-start | bytes 3145736 | tf_op jit(solution)/shard_map/ppermute | solution.py:223
  91.2 52.7 %collective-permute-start.34 = (f32[256,2048]{1,0:T(8,128)}, f32[256,2048]{1,0:T(8,128)S(1)}, u32[]{:S(2)}, u32[]{:S(2)}) collective-permute-start(f32[256,2048]{1,0:T(8,128)} %get-tuple-element.59), channel_id=1, source_target_pairs={{0,1},{1,0},{2,3},{3,2},{4,5},{5,4},{6,7},{7,6},{8,9},{9,8},{10,11... | collective-permute-start | bytes 6291464 | tf_op jit(solution)/shard_map/ppermute | solution.py:226
  143.3 29.1 %collective-permute-start.33 = (bf16[128,4096]{1,0:T(8,128)(2,1)}, bf16[128,4096]{1,0:T(8,128)(2,1)S(1)}, u32[]{:S(2)}, u32[]{:S(2)}) collective-permute-start(bf16[128,4096]{1,0:T(8,128)(2,1)} %collective-permute-done.10.refs_0_), channel_id=1, source_target_pairs={{0,4},{4,0},{8,12},{12,8},{16,20},{20,16},{24,28},{28,24},{1,5},{5... | collective-permute-start | bytes 3145736 | tf_op jit(solution)/shard_map/ppermute | solution.py:223
  143.9 31.1 %collective-permute-start.32 = (bf16[128,4096]{1,0:T(8,128)(2,1)}, bf16[128,4096]{1,0:T(8,128)(2,1)}, u32[]{:S(2)}, u32[]{:S(2)}) collective-permute-start(bf16[128,4096]{1,0:T(8,128)(2,1)} %collective-permute-done.10.refs_0_), channel_id=1, source_target_pairs={{0,8},{4,12},{8,16},{12,20},{16,24},{20,28},{24,0},{28,4},{1,9},{5... | collective-permute-start | bytes 3145736 | tf_op jit(solution)/shard_map/ppermute | solution.py:223
  144.0 26.1 %collective-permute-start.35 = (f32[128,2048]{1,0:T(8,128)S(1)}, f32[128,2048]{1,0:T(8,128)S(1)}, u32[]{:S(2)}, u32[]{:S(2)}) collective-permute-start(f32[128,2048]{1,0:T(8,128)S(1)} %slice_add_fusion), channel_id=1, source_target_pairs={{0,2},{1,3},{2,0},{3,1},{4,6},{5,7},{6,4},{7,5},{8,10},{9,11},{10,... | collective-permute-start | bytes 3145736 | tf_op jit(solution)/shard_map/ppermute | solution.py:226
  148.0 44.6 %collective-permute-start.13 = (f32[128,2048]{1,0:T(8,128)}, f32[128,2048]{1,0:T(8,128)}, u32[]{:S(2)}, u32[]{:S(2)}) collective-permute-start(f32[128,2048]{1,0:T(8,128)} %slice_add_fusion.2), channel_id=1, source_target_pairs={{0,2},{1,3},{2,0},{3,1},{4,6},{5,7},{6,4},{7,5},{8,10},{9,11},{10,... | collective-permute-start | bytes 3145736 | tf_op jit(solution)/shard_map/ppermute | solution.py:226
  149.9 47.1 %collective-permute-start.7 = (bf16[128,4096]{1,0:T(8,128)(2,1)}, bf16[128,4096]{1,0:T(8,128)(2,1)}, u32[]{:S(2)}, u32[]{:S(2)}) collective-permute-start(bf16[128,4096]{1,0:T(8,128)(2,1)} %collective-permute-done.2.refs_2_), channel_id=1, source_target_pairs={{0,4},{4,0},{8,12},{12,8},{16,20},{20,16},{24,28},{28,24},{1,5},{5... | collective-permute-start | bytes 3145736 | tf_op jit(solution)/shard_map/ppermute | solution.py:223
  170.1 28.6 %collective-permute-start.6 = (bf16[128,4096]{1,0:T(8,128)(2,1)}, bf16[128,4096]{1,0:T(8,128)(2,1)}, u32[]{:S(2)}, u32[]{:S(2)}) collective-permute-start(bf16[128,4096]{1,0:T(8,128)(2,1)} %collective-permute-done.2.refs_2_), channel_id=1, source_target_pairs={{0,8},{4,12},{8,16},{12,20},{16,24},{20,28},{24,0},{28,4},{1,9},{5... | collective-permute-start | bytes 3145736 | tf_op jit(solution)/shard_map/ppermute | solution.py:223
  173.5 39.6 %collective-permute-start.50 = (bf16[128,2048]{1,0:T(8,128)(2,1)S(1)}, bf16[128,2048]{1,0:T(8,128)(2,1)S(1)}, u32[]{:S(2)}, u32[]{:S(2)}) collective-permute-start(bf16[128,2048]{1,0:T(8,128)(2,1)S(1)} %get-tuple-element.76), channel_id=1, source_target_pairs={{0,2},{1,3},{2,0},{3,1},{4,6},{5,7},{6,4},{7,5},{8,10},{9,11},{10,... | collective-permute-start | bytes 1572872 | tf_op jit(solution)/shard_map/ppermute | solution.py:226
  185.4 30.5 %collective-permute-start.38 = (f32[128,2048]{1,0:T(8,128)}, f32[128,2048]{1,0:T(8,128)}, u32[]{:S(2)}, u32[]{:S(2)}) collective-permute-start(f32[128,2048]{1,0:T(8,128)} %get-tuple-element.64), channel_id=1, source_target_pairs={{0,1},{1,0},{2,3},{3,2},{4,5},{5,4},{6,7},{7,6},{8,9},{9,8},{10,11... | collective-permute-start | bytes 3145736 | tf_op jit(solution)/shard_map/ppermute | solution.py:226
  194.9 20.4 %collective-permute-start.44 = (bf16[128,2048]{1,0:T(8,128)(2,1)S(1)}, bf16[128,2048]{1,0:T(8,128)(2,1)S(1)}, u32[]{:S(2)}, u32[]{:S(2)}) collective-permute-start(bf16[128,2048]{1,0:T(8,128)(2,1)S(1)} %get-tuple-element.74), channel_id=1, source_target_pairs={{0,2},{1,3},{2,0},{3,1},{4,6},{5,7},{6,4},{7,5},{8,10},{9,11},{10,... | collective-permute-start | bytes 1572872 | tf_op jit(solution)/shard_map/ppermute | solution.py:226
  197.1 37.6 %collective-permute-start.36 = (bf16[128,4096]{1,0:T(8,128)(2,1)}, bf16[128,4096]{1,0:T(8,128)(2,1)S(1)}, u32[]{:S(2)}, u32[]{:S(2)}) collective-permute-start(bf16[128,4096]{1,0:T(8,128)(2,1)} %collective-permute-done.32.refs_0_), channel_id=1, source_target_pairs={{0,4},{4,0},{8,12},{12,8},{16,20},{20,16},{24,28},{28,24},{1,5},{5... | collective-permute-start | bytes 3145736 | tf_op jit(solution)/shard_map/ppermute | solution.py:223
  198.6 36.0 %collective-permute-start.37 = (bf16[128,4096]{1,0:T(8,128)(2,1)}, bf16[128,4096]{1,0:T(8,128)(2,1)S(1)}, u32[]{:S(2)}, u32[]{:S(2)}) collective-permute-start(bf16[128,4096]{1,0:T(8,128)(2,1)} %copy-done.7), channel_id=1, source_target_pairs={{0,24},{4,28},{8,0},{12,4},{16,8},{20,12},{24,16},{28,20},{1,25},{... | collective-permute-start | bytes 3145736 | tf_op jit(solution)/shard_map/ppermute | solution.py:223
  215.3 36.6 %collective-permute-start.51 = (bf16[256,2048]{1,0:T(8,128)(2,1)}, bf16[256,2048]{1,0:T(8,128)(2,1)}, u32[]{:S(2)}, u32[]{:S(2)}) collective-permute-start(bf16[256,2048]{1,0:T(8,128)(2,1)} %pad_maximum_fusion.3), channel_id=1, source_target_pairs={{0,1},{1,0},{2,3},{3,2},{4,5},{5,4},{6,7},{7,6},{8,9},{9,8},{10,11... | collective-permute-start | bytes 3145736 | tf_op jit(solution)/shard_map/ppermute | solution.py:226
  219.7 28.3 %collective-permute-start.20 = (bf16[1392,128]{1,0:T(8,128)(2,1)S(1)}, bf16[1392,128]{1,0:T(8,128)(2,1)}, u32[]{:S(2)}, u32[]{:S(2)}) collective-permute-start(bf16[1392,128]{1,0:T(8,128)(2,1)S(1)} %slice.119.refs_0_), channel_id=1, source_target_pairs={{0,8},{4,12},{8,16},{12,20},{16,24},{20,28},{24,0},{28,4},{1,9},{5... | collective-permute-start | bytes 1069064 | tf_op jit(solution)/shard_map/ppermute | solution.py:223
  232.3 29.0 %collective-permute-start.29 = (f32[64,2048]{1,0:T(8,128)}, f32[64,2048]{1,0:T(8,128)}, u32[]{:S(2)}, u32[]{:S(2)}) collective-permute-start(f32[64,2048]{1,0:T(8,128)} %slice_add_fusion.8), channel_id=1, source_target_pairs={{0,2},{1,3},{2,0},{3,1},{4,6},{5,7},{6,4},{7,5},{8,10},{9,11},{10,... | collective-permute-start | bytes 1572872 | tf_op jit(solution)/shard_map/ppermute | solution.py:226
  252.0 25.2 %collective-permute-start.14 = (bf16[1408,128]{1,0:T(8,128)(2,1)S(1)}, bf16[1408,128]{1,0:T(8,128)(2,1)S(1)}, u32[]{:S(2)}, u32[]{:S(2)}) collective-permute-start(bf16[1408,128]{1,0:T(8,128)(2,1)S(1)} %slice.118.refs_0_), channel_id=1, source_target_pairs={{0,8},{4,12},{8,16},{12,20},{16,24},{20,28},{24,0},{28,4},{1,9},{5... | collective-permute-start | bytes 1081352 | tf_op jit(solution)/shard_map/ppermute | solution.py:223
  265.8 20.0 %collective-permute-start.41 = (f32[64,2048]{1,0:T(8,128)S(1)}, f32[64,2048]{1,0:T(8,128)S(1)}, u32[]{:S(2)}, u32[]{:S(2)}) collective-permute-start(f32[64,2048]{1,0:T(8,128)S(1)} %slice_add_fusion.4), channel_id=1, source_target_pairs={{0,2},{1,3},{2,0},{3,1},{4,6},{5,7},{6,4},{7,5},{8,10},{9,11},{10,... | collective-permute-start | bytes 1572872 | tf_op jit(solution)/shard_map/ppermute | solution.py:226
  277.2 26.1 %collective-permute-start.25 = (bf16[1392,128]{1,0:T(8,128)(2,1)}, bf16[1392,128]{1,0:T(8,128)(2,1)S(1)}, u32[]{:S(2)}, u32[]{:S(2)}) collective-permute-start(bf16[1392,128]{1,0:T(8,128)(2,1)} %collective-permute-done.20.refs_1_), channel_id=1, source_target_pairs={{0,4},{4,0},{8,12},{12,8},{16,20},{20,16},{24,28},{28,24},{1,5},{5... | collective-permute-start | bytes 1069064 | tf_op jit(solution)/shard_map/ppermute | solution.py:223
  278.3 25.9 %collective-permute-start.16 = (bf16[1408,128]{1,0:T(8,128)(2,1)S(1)}, bf16[1408,128]{1,0:T(8,128)(2,1)S(1)}, u32[]{:S(2)}, u32[]{:S(2)}) collective-permute-start(bf16[1408,128]{1,0:T(8,128)(2,1)S(1)} %collective-permute-done.14.refs_1_), channel_id=1, source_target_pairs={{0,8},{4,12},{8,16},{12,20},{16,24},{20,28},{24,0},{28,4},{1,9},{5... | collective-permute-start | bytes 1081352 | tf_op jit(solution)/shard_map/ppermute | solution.py:223
  303.3 51.8 %collective-permute-start.17 = (bf16[1408,128]{1,0:T(8,128)(2,1)S(1)}, bf16[1408,128]{1,0:T(8,128)(2,1)S(1)}, u32[]{:S(2)}, u32[]{:S(2)}) collective-permute-start(bf16[1408,128]{1,0:T(8,128)(2,1)S(1)} %collective-permute-done.14.refs_1_), channel_id=1, source_target_pairs={{0,4},{4,0},{8,12},{12,8},{16,20},{20,16},{24,28},{28,24},{1,5},{5... | collective-permute-start | bytes 1081352 | tf_op jit(solution)/shard_map/ppermute | solution.py:223
  304.3 50.9 %collective-permute-start.19 = (bf16[1408,128]{1,0:T(8,128)(2,1)S(1)}, bf16[1408,128]{1,0:T(8,128)(2,1)S(1)}, u32[]{:S(2)}, u32[]{:S(2)}) collective-permute-start(bf16[1408,128]{1,0:T(8,128)(2,1)S(1)} %collective-permute-done.16.refs_3_), channel_id=1, source_target_pairs={{0,4},{4,0},{8,12},{12,8},{16,20},{20,16},{24,28},{28,24},{1,5},{5... | collective-permute-start | bytes 1081352 | tf_op jit(solution)/shard_map/ppermute | solution.py:223
  305.4 49.7 %collective-permute-start.18 = (bf16[1408,128]{1,0:T(8,128)(2,1)S(1)}, bf16[1408,128]{1,0:T(8,128)(2,1)S(1)}, u32[]{:S(2)}, u32[]{:S(2)}) collective-permute-start(bf16[1408,128]{1,0:T(8,128)(2,1)S(1)} %collective-permute-done.16.refs_3_), channel_id=1, source_target_pairs={{0,8},{4,12},{8,16},{12,20},{16,24},{20,28},{24,0},{28,4},{1,9},{5... | collective-permute-start | bytes 1081352 | tf_op jit(solution)/shard_map/ppermute | solution.py:223
  305.4 49.7 %collective-permute-start.23 = (bf16[1408,128]{1,0:T(8,128)(2,1)S(1)}, bf16[1408,128]{1,0:T(8,128)(2,1)S(1)}, u32[]{:S(2)}, u32[]{:S(2)}) collective-permute-start(bf16[1408,128]{1,0:T(8,128)(2,1)S(1)} %collective-permute-done.15.refs_2_), channel_id=1, source_target_pairs={{0,24},{4,28},{8,0},{12,4},{16,8},{20,12},{24,16},{28,20},{1,25},{... | collective-permute-start | bytes 1081352 | tf_op jit(solution)/shard_map/ppermute | solution.py:223
  (55 other events, 789.3 us)

commit v2 on v1

--- a/solution.py
+++ b/solution.py
@@ -8,6 +8,7 @@
 from jax.sharding import PartitionSpec as P
 
 OCC_B = 2
+COEF_AT = 2
 LAGS = (None, None, 1, None)
 VMEM_LIMIT = 56 * 1024 * 1024
 BF16, F32 = jnp.bfloat16, jnp.float32
@@ -76,7 +77,7 @@
         ],
         compiler_params=params(),
         cost_estimate=pl.CostEstimate(
-            flops=0, bytes_accessed=0, transcendentals=0
+            flops=1000, bytes_accessed=1000, transcendentals=0
         ),
         name="first_product",
     )(place, lhs, resolvent)
@@ -117,7 +118,7 @@
         out_shape=[jax.ShapeDtypeStruct((half, cols), F32)] * 2,
         compiler_params=params(),
         cost_estimate=pl.CostEstimate(
-            flops=0, bytes_accessed=0, transcendentals=0
+            flops=1000, bytes_accessed=1000, transcendentals=0
         ),
         name="group_product",
     )(place, *pieces, r16)
@@ -136,7 +137,7 @@
     @pl.when(pl.program_id(0) == 0)
     def _():
         at = 0
-        for c in coefs:
+        for c in coefs if n > 1 else ():
             lhs[:, at : at + c.shape[1]] = c[...]
             at += c.shape[1]
         at = 0
@@ -158,7 +159,8 @@
                 )
                 at += wide
             whole_ref[o] = placed.astype(BF16)
-        out_ref[o] = jnp.dot(lhs[...], whole_ref[o], preferred_element_type=F32)
+        left = lhs if n > 1 else coefs[0]
+        out_ref[o] = jnp.dot(left[...], whole_ref[o], preferred_element_type=F32)
 
 
 def back_product(coefs, late, grouped, total, first, out):
@@ -171,7 +173,7 @@
     whole = (pl.Element(occ), pl.Element(chunk), pl.Element(tile))
     out_specs = [pl.BlockSpec(whole, lambda i: (0, first, i * tile))]
     shapes = [jax.ShapeDtypeStruct((occ, total, cols), F32)]
-    scratch = [pltpu.VMEM((chunk, depth), BF16)]
+    scratch = [pltpu.VMEM((chunk, depth) if n > 1 else (8, 128), BF16)]
     args = list(coefs)
     aliases = {}
     if late is not None:
@@ -199,7 +201,7 @@
         input_output_aliases=aliases,
         compiler_params=params(),
         cost_estimate=pl.CostEstimate(
-            flops=0, bytes_accessed=0, transcendentals=0
+            flops=1000, bytes_accessed=1000, transcendentals=0
         ),
         name="back_product",
     )(*args)
@@ -228,35 +230,7 @@
     def block_of(s, cross):
         return (me_row // 2 + (high - s)) % high * 2 + ((me_row % 2) ^ cross)
 
-    def spread(pieces, fence):
-        straight = [dict(enumerate(pieces))]
-        crossed = []
-        arrivals = []
-        for s in range(high - 1):
-            straight.append({})
-            crossed.append({})
-            for c in range(2):
-                got = [over_rows(straight[s][c], up), over_rows(straight[s][c], swap)]
-                straight[s + 1][c], crossed[s][c] = got = fence(got)
-                arrivals.append([((s + 1, 0, c), got[0]), ((s, 1, c), got[1])])
-        s = high - 1
-        ends = [over_rows(straight[s][0], swap)]
-        if high > 1:
-            ends.append(over_rows(tied(crossed[0][1], straight[s][0]), down))
-        else:
-            ends.append(over_rows(straight[s][1], swap))
-        ends = fence(ends)
-        arrivals.append([((s, 1, c), ends[c]) for c in range(2)])
-        return arrivals
-
-    vblock = virt_coef.shape[0]
-    sequence = [(0, 0)] + [
-        key for s in range(high) for key in ([(s + 1, 0)] if s < high - 1 else []) + [(s, 1)]
-    ]
-    by_block = slot_row.reshape(OCC_B, rows, vblock)
-    slots = jnp.concatenate(
-        [lax.dynamic_slice_in_dim(by_block, block_of(*key), 1, axis=1) for key in sequence], axis=1
-    ).reshape(-1, 1)
+    slots = slot_row.reshape(-1, 1)
 
     size = pair_block.shape[0]
     step = size // 2
@@ -304,7 +278,6 @@
     grouped = None
     count = 2 * (high - 1) + 1
     batch = max(1, 512 // (2 * step))
-    closing = [len(range(0, h + 1)) for h in range(count)]
     closes = {h for h in range(count) if h >= count - 3 or (h + 1) % batch == 0 or h == count - 4}
     pending = []
     marks = []
@@ -319,9 +292,6 @@
         got = list(lax.optimization_barrier((*got, *after)))[: len(got)]
         marks.append(got[0])
         return got
-
-    coef_at = max(count - 2, 0)
-    arrivals = None
 
     state = {"grouped": None}
 
@@ -356,34 +326,17 @@
     ends = fence(ends)
     take(h, [((s, 1, c), ends[c]) for c in range(2)])
 
+    coef_all = lax.all_gather(tied(virt_coef, marks[min(COEF_AT, count - 1)]), "rows", axis=0, tiled=True)
     done = len(gammas) - 2 if len(gammas) % 2 == 0 else len(gammas) - 1
     late = list(range(0 if state["grouped"] is None else done, len(gammas)))
     grouped = state["grouped"]
     if grouped is None:
         grouped = jnp.zeros((slots.shape[0], gammas[0].shape[1]), BF16)
 
-    coef = tied(virt_coef, marks[max(len(marks) - 2, 0)]).T
-    total = coef.shape[0]
-    cut = divisor_tile(total, 16, total // 2)
-    cut = total // 16 // 2 * 16
-    arrived = [{}, {}]
-    for items in spread([coef[:cut], coef[cut:]], lambda got: got):
-        for (back, x, c), v in items:
-            arrived[c][(back, x)] = v
-    arrived[0][(0, 0)], arrived[1][(0, 0)] = coef[:cut], coef[cut:]
-    grouped = grouped.reshape(OCC_B, rows * vblock, -1)
-    out = None
-    for c, first in enumerate((0, cut)):
-        parts = [arrived[c][key] for key in sequence]
-        if vblock % 128:
-            parts = [jnp.concatenate(parts, axis=1)]
-        if c == 0:
-            out, grouped = back_product(
-                parts, (slots, [ids[k] for k in late], [gammas[k] for k in late]), grouped, total, first, None
-            )
-        else:
-            (out,) = back_product(parts, None, grouped, total, first, out)
-    return out
+    coef = coef_all.T
+    grouped = grouped.reshape(OCC_B, coef.shape[1], -1)
+    late_rows = (slots, [ids[k] for k in late], [gammas[k] for k in late])
+    return back_product([coef], late_rows, grouped, coef.shape[0], 0, None)[0]
 
 
 def solution(mesh):

time: 377 us -> 358 us (0.950)
  starting transfers between devices: 45.2 us -> 31.2 us
  between operations: 0.64 us -> 13.9 us
  waiting for transfers between devices: 149 us -> 141 us
  Pallas kernels: 125 us -> 120 us
  local copies, waits for them, and re-layouts: 18.8 us -> 14 us
    ppermute x28 -> x14, waiting for transfers between devices: 93.6 us -> 78.3 us  [over_rows(): return lax.ppermute(v, 'rows', pairs)]
    ppermute x28 -> x14, starting transfers between devices: 29.2 us -> 15.6 us  [over_rows(): return lax.ppermute(v, 'rows', pairs)]
    ppermute x24, waiting for transfers between devices: 55.2 us -> 61.1 us  [over_panel(): return lax.ppermute(v, 'panel', [(q, q ^ width) for q in range(panel)])]
    pallas_call x2 -> x1, Pallas kernels: 44.6 us -> 40.2 us  [back_product(): pl.pallas_call(functools.partial(back_kernel, n, m), grid=(cols // tile,)...]
    unnamed x76 -> x44, local copies, waits for them, and re-layouts: 10.7 us -> 8.05 us
  transfers between devices with their start and end apart: 52 -> 39, of which waited for: 16 -> 19; matrix products, arithmetic and copies ran while one was open for 13% -> 13% of each run, Pallas kernels for 23% -> 17%
where the time goes in v2:
time: 358 us; the launch traced here: 357 us
  waiting for transfers between devices  141 us (39%)
  Pallas kernels  120 us (34%)
  starting transfers between devices  31.2 us (9%)
  matrix products  18.5 us (5%)
  other arithmetic  18.3 us (5%)
  local copies, waits for them, and re-layouts  14 us (4%)
  between operations  13.9 us (4%)
    ppermute x14, waiting for transfers between devices, over_rows(): return lax.ppermute(v, 'rows', pairs)  78.3 us
    ppermute x24, waiting for transfers between devices, over_panel(): return lax.ppermute(v, 'panel', [(q, q ^ width) for q in range(panel)])  61.1 us
    pallas_call x5, Pallas kernels, group_product(): pl.pallas_call(functools.partial(group_kernel, len(pieces), order), grid_...  60.6 us
    pallas_call x1, Pallas kernels, back_product(): pl.pallas_call(functools.partial(back_kernel, n, m), grid=(cols // tile,)...  40.2 us
    pallas_call x1, Pallas kernels, first_product(): pl.pallas_call(functools.partial(first_kernel, order), grid_spec=pltpu.Pr...  19.6 us
    dot_general x2, matrix products, regroup(): placed = jnp.dot(pick, gamma, preferred_element_type=F32)  18.5 us
    ppermute x24, starting transfers between devices, over_panel(): return lax.ppermute(v, 'panel', [(q, q ^ width) for q in range(panel)])  15.6 us
    ppermute x14, starting transfers between devices, over_rows(): return lax.ppermute(v, 'rows', pairs)  15.6 us
  transfers between devices with their start and end apart: 39, of which 19 were waited for; matrix products, arithmetic and copies ran while one was open for 13% of the time, Pallas kernels for 17%

profile of v2, /device:TPU:0, one launch (start us, length us, event | category | flops | bytes accessed | tf_op | source)
XLA Modules:
  0.0 357.2 jit_solution(10026051630515719175)
XLA Ops:
  6.5 19.6 %first_product.1 = (bf16[4096,2048]{1,0:T(8,128)(2,1)}, f32[128,2048]{1,0:T(8,128)}, f32[128,2048]{1,0:T(8,128)}) custom-call(s32[1]{0:T(128)} %bitcast.place_ref, bf16[256,4096]{1,0:T(8,128)(2,1)} %lhs_ref.1, f32[4096,2048]{1,0:T(8,128)} %r_ref.1), custom_call_target="tpu_custom_call" | custom-call | flops 1000 | bytes 1000 | tf_op jit(solution)/shard_map/first_product/pallas_call | solution.py:57
  28.7 2.5 collective-permute-start.7
  31.3 1.6 collective-permute-start.6
  33.3 1.6 collective-permute-start
  37.8 17.6 %collective-permute-done.7.refs_3_ = bf16[128,4096]{1,0:T(8,128)(2,1)S(1)} collective-permute-done((bf16[128,4096]{1,0:T(8,128)(2,1)}, bf16[128,4096]{1,0:T(8,128)(2,1)S(1)}, u32[]{:S(2)}, u32[]{:S(2)}) %collective-permute-start.7) | collective-permute-done | bytes 1048608 | tf_op jit(solution)/shard_map/ppermute | solution.py:225
  55.5 3.8 %collective-permute-done.6.refs_2_ = bf16[128,4096]{1,0:T(8,128)(2,1)S(1)} collective-permute-done((bf16[128,4096]{1,0:T(8,128)(2,1)}, bf16[128,4096]{1,0:T(8,128)(2,1)S(1)}, u32[]{:S(2)}, u32[]{:S(2)}) %collective-permute-start.6) | collective-permute-done | bytes 1048608 | tf_op jit(solution)/shard_map/ppermute | solution.py:225
  59.6 18.4 %collective-permute-done.1.refs_1_ = bf16[128,4096]{1,0:T(8,128)(2,1)S(1)} collective-permute-done((bf16[128,4096]{1,0:T(8,128)(2,1)}, bf16[128,4096]{1,0:T(8,128)(2,1)S(1)}, u32[]{:S(2)}, u32[]{:S(2)}) %collective-permute-start.1) | collective-permute-done | bytes 1048608 | tf_op jit(solution)/shard_map/ppermute | solution.py:225
  78.0 3.9 %collective-permute-done.refs_0_ = bf16[128,4096]{1,0:T(8,128)(2,1)} collective-permute-done((bf16[128,4096]{1,0:T(8,128)(2,1)}, bf16[128,4096]{1,0:T(8,128)(2,1)}, u32[]{:S(2)}, u32[]{:S(2)}) %collective-permute-start) | collective-permute-done | bytes 1048608 | tf_op jit(solution)/shard_map/ppermute | solution.py:225
  82.2 14.6 %group_product.7 = (f32[256,2048]{1,0:T(8,128)}, f32[256,2048]{1,0:T(8,128)}) custom-call(s32[1]{0:T(128)} %bitcast.place_ref, bf16[128,4096]{1,0:T(8,128)(2,1)} %collective-permute-done.refs_0_, bf16[128,4096]{1,0:T(8,128)(2,1)} %copy-done.7, bf16[128,4096]{1,0:T(8,128)(2,1)} %copy-done.6, bf16[128,4096]{1,0:T(8,128)(2,1)} %copy-done.5, ...), custom_call_target="tpu_custom_call" | custom-call | flops 1000 | bytes 1000 | tf_op jit(solution)/shard_map/group_product/pallas_call | solution.py:105
  96.9 2.2 constant_dynamic-update-slice_fusion.11
  100.5 3.8 %collective-permute-done.8.refs_2_ = bf16[128,4096]{1,0:T(8,128)(2,1)} collective-permute-done((bf16[128,4096]{1,0:T(8,128)(2,1)S(1)}, bf16[128,4096]{1,0:T(8,128)(2,1)}, u32[]{:S(2)}, u32[]{:S(2)}) %collective-permute-start.8) | collective-permute-done | bytes 1048608 | tf_op jit(solution)/shard_map/ppermute | solution.py:225
  104.3 18.5 %collective-permute-done.3.refs_1_ = bf16[128,4096]{1,0:T(8,128)(2,1)} collective-permute-done((bf16[128,4096]{1,0:T(8,128)(2,1)}, bf16[128,4096]{1,0:T(8,128)(2,1)}, u32[]{:S(2)}, u32[]{:S(2)}) %collective-permute-start.3) | collective-permute-done | bytes 1048608 | tf_op jit(solution)/shard_map/ppermute | solution.py:225
  122.8 3.4 collective-permute-done.2.refs_0_
  126.2 14.5 %group_product.5 = (f32[256,2048]{1,0:T(8,128)}, f32[256,2048]{1,0:T(8,128)}) custom-call(s32[1]{0:T(128)} %bitcast.place_ref, bf16[128,4096]{1,0:T(8,128)(2,1)} %collective-permute-done.2.refs_0_, bf16[128,4096]{1,0:T(8,128)(2,1)} %collective-permute-done.3.refs_1_, bf16[128,4096]{1,0:T(8,128)(2,1)} %collective-permute-done.8.refs_2_, ...), custom_call_target="tpu_custom_call" | custom-call | flops 1000 | bytes 1000 | tf_op jit(solution)/shard_map/group_product/pallas_call | solution.py:105
  143.1 6.5 %collective-permute-done.34 = bf16[64,2048]{1,0:T(8,128)(2,1)S(1)} collective-permute-done((bf16[64,2048]{1,0:T(8,128)(2,1)S(1)}, bf16[64,2048]{1,0:T(8,128)(2,1)S(1)}, u32[]{:S(2)}, u32[]{:S(2)}) %collective-permute-start.34) | collective-permute-done | bytes 262176 | tf_op jit(solution)/shard_map/ppermute | solution.py:228
  158.1 18.4 %collective-permute-done.21 = f32[128,2048]{1,0:T(8,128)S(1)} collective-permute-done((f32[128,2048]{1,0:T(8,128)S(1)}, f32[128,2048]{1,0:T(8,128)S(1)}, u32[]{:S(2)}, u32[]{:S(2)}) %collective-permute-start.21) | collective-permute-done | bytes 1048608 | tf_op jit(solution)/shard_map/ppermute | solution.py:228
  181.3 10.5 %group_product.8 = (f32[128,2048]{1,0:T(8,128)}, f32[128,2048]{1,0:T(8,128)}) custom-call(s32[1]{0:T(128)} %bitcast.place_ref, bf16[128,4096]{1,0:T(8,128)(2,1)} %collective-permute-done.18.refs_0_, bf16[128,4096]{1,0:T(8,128)(2,1)} %copy-done.16, bf16[4096,2048]{1,0:T(8,128)(2,1)} %get-tuple-element.46.refs_4_.refs_2_), custom_call_target="tpu_custom_call" | custom-call | flops 1000 | bytes 1000 | tf_op jit(solution)/shard_map/group_product/pallas_call | solution.py:105
  191.8 7.3 %collective-permute-done.13 = f32[128,2048]{1,0:T(8,128)} collective-permute-done((f32[128,2048]{1,0:T(8,128)}, f32[128,2048]{1,0:T(8,128)}, u32[]{:S(2)}, u32[]{:S(2)}) %collective-permute-start.13) | collective-permute-done | bytes 1048608 | tf_op jit(solution)/shard_map/ppermute | solution.py:228
  199.0 2.2 constant_dynamic-update-slice_fusion.5
  202.9 1.6 collective-permute-start.22
  204.5 3.9 %collective-permute-start.23 = (bf16[128,4096]{1,0:T(8,128)(2,1)}, bf16[128,4096]{1,0:T(8,128)(2,1)S(1)}, u32[]{:S(2)}, u32[]{:S(2)}) collective-permute-start(bf16[128,4096]{1,0:T(8,128)(2,1)} %copy-done.5), channel_id=1, source_target_pairs={{0,24},{4,28},{8,0},{12,4},{16,8},{20,12},{24,16},{28,20},{1,25},{... | collective-permute-start | bytes 3145736 | tf_op jit(solution)/shard_map/ppermute | solution.py:225
  208.4 10.6 %group_product.6 = (f32[128,2048]{1,0:T(8,128)}, f32[128,2048]{1,0:T(8,128)}) custom-call(s32[1]{0:T(128)} %bitcast.place_ref, bf16[128,4096]{1,0:T(8,128)(2,1)} %collective-permute-done.10.refs_0_, bf16[128,4096]{1,0:T(8,128)(2,1)} %collective-permute-done.11.refs_1_, bf16[4096,2048]{1,0:T(8,128)(2,1)} %get-tuple-element.46.refs_4_.refs_2_), custom_call_target="tpu_custom_call" | custom-call | flops 1000 | bytes 1000 | tf_op jit(solution)/shard_map/group_product/pallas_call | solution.py:105
  227.4 9.6 %collective-permute-done.25 = f32[64,2048]{1,0:T(8,128)S(1)} collective-permute-done((f32[64,2048]{1,0:T(8,128)S(1)}, f32[64,2048]{1,0:T(8,128)S(1)}, u32[]{:S(2)}, u32[]{:S(2)}) %collective-permute-start.25) | collective-permute-done | bytes 524320 | tf_op jit(solution)/shard_map/ppermute | solution.py:228
  237.8 7.5 %collective-permute-done.23.refs_1_ = bf16[128,4096]{1,0:T(8,128)(2,1)S(1)} collective-permute-done((bf16[128,4096]{1,0:T(8,128)(2,1)}, bf16[128,4096]{1,0:T(8,128)(2,1)S(1)}, u32[]{:S(2)}, u32[]{:S(2)}) %collective-permute-start.23) | collective-permute-done | bytes 1048608 | tf_op jit(solution)/shard_map/ppermute | solution.py:225
  246.7 10.4 %group_product.9 = (f32[128,2048]{1,0:T(8,128)}, f32[128,2048]{1,0:T(8,128)}) custom-call(s32[1]{0:T(128)} %bitcast.place_ref, bf16[128,4096]{1,0:T(8,128)(2,1)} %copy-done.14, bf16[128,4096]{1,0:T(8,128)(2,1)} %copy-done.15, bf16[4096,2048]{1,0:T(8,128)(2,1)} %get-tuple-element.46.refs_4_.refs_2_), custom_call_target="tpu_custom_call" | custom-call | flops 1000 | bytes 1000 | tf_op jit(solution)/shard_map/group_product/pallas_call | solution.py:105
  260.0 2.4 constant_dynamic-update-slice_fusion.6
  263.5 2.1 collective-permute-start.16
  266.8 9.3 %fusion = bf16[2048,2048]{1,0:T(8,128)(2,1)S(1)} fusion(bf16[768,2048]{1,0:T(8,128)(2,1)} %constant_dynamic-update-slice_fusion.6, s32[768]{0:T(1024)S(1)} %add_reduce_fusion.1, s32[2048]{0:T(1024)S(1)} %copy-done.18), kind=kOutput, calls=%fused_computation.1 | convolution fusion | flops 6444023808 | bytes 11545600 | tf_op jit(solution)/shard_map/dot_general | solution.py:269
  277.8 10.1 %collective-permute-done.27 = f32[64,2048]{1,0:T(8,128)S(1)} collective-permute-done((f32[64,2048]{1,0:T(8,128)S(1)}, f32[64,2048]{1,0:T(8,128)S(1)}, u32[]{:S(2)}, u32[]{:S(2)}) %collective-permute-start.27) | collective-permute-done | bytes 524320 | tf_op jit(solution)/shard_map/ppermute | solution.py:228
  289.5 7.7 %collective-permute-done.28 = bf16[64,2048]{1,0:T(8,128)(2,1)S(1)} collective-permute-done((bf16[64,2048]{1,0:T(8,128)(2,1)S(1)}, bf16[64,2048]{1,0:T(8,128)(2,1)S(1)}, u32[]{:S(2)}, u32[]{:S(2)}) %collective-permute-start.28) | collective-permute-done | bytes 262176 | tf_op jit(solution)/shard_map/ppermute | solution.py:228
  297.3 9.1 %add_convert_fusion = bf16[2048,2048]{1,0:T(8,128)(2,1)} fusion(bf16[2048,2048]{1,0:T(8,128)(2,1)S(1)} %fusion, bf16[768,2048]{1,0:T(8,128)(2,1)S(1)} %constant_dynamic-update-slice_fusion, s32[768]{0:T(1024)S(1)} %add_reduce_fusion, s32[2048]{0:T(1024)S(1)} %copy-done.18), kind=kOutput, calls=%fused_computation | convolution fusion | flops 6456606720 | bytes 19934208 | tf_op jit(solution)/shard_map/dot_general | solution.py:269
  310.1 40.2 %back_product.1 = (f32[2,2800,2048]{2,1,0:T(8,128)}, bf16[2,1024,2048]{2,1,0:T(8,128)(2,1)}) custom-call(bf16[2800,1024]{1,0:T(8,128)(2,1)} %bitcast.65, s32[2048,1]{1,0:T(8,128)} %copy.5.refs_1_, s32[1,256]{1,0:T(1,128)} %bitcast.69, s32[1,256]{1,0:T(1,128)} %bitcast.70, bf16[256,2048]{1,0:T(8,128)(2,1)} %pad_maximum_fusion.refs_4_, ...), custom_call_target="tpu_custom_call" | custom-call | flops 1000 | bytes 1000 | tf_op jit(solution)/shard_map/back_product/pallas_call | solution.py:194
  (158 shorter events, 48.2 us)
Async XLA Ops:
  6.5 303.6 %all-gather.2.cloned.1.call-start = ((), (), s32[]{:S(2)}) async-start(), calls=%async_computation | async-start | bytes 6451200 | tf_op jit(solution)/shard_map/all_gather | solution.py:329
  28.7 26.7 %collective-permute-start.7 = (bf16[128,4096]{1,0:T(8,128)(2,1)}, bf16[128,4096]{1,0:T(8,128)(2,1)S(1)}, u32[]{:S(2)}, u32[]{:S(2)}) collective-permute-start(bf16[128,4096]{1,0:T(8,128)(2,1)} %slice.83), channel_id=1, source_target_pairs={{0,4},{4,0},{8,12},{12,8},{16,20},{20,16},{24,28},{28,24},{1,5},{5... | collective-permute-start | bytes 3145736 | tf_op jit(solution)/shard_map/ppermute | solution.py:225
  31.3 28.0 %collective-permute-start.6 = (bf16[128,4096]{1,0:T(8,128)(2,1)}, bf16[128,4096]{1,0:T(8,128)(2,1)S(1)}, u32[]{:S(2)}, u32[]{:S(2)}) collective-permute-start(bf16[128,4096]{1,0:T(8,128)(2,1)} %slice.83), channel_id=1, source_target_pairs={{0,8},{4,12},{8,16},{12,20},{16,24},{20,28},{24,0},{28,4},{1,9},{5... | collective-permute-start | bytes 3145736 | tf_op jit(solution)/shard_map/ppermute | solution.py:225
  32.8 45.1 %collective-permute-start.1 = (bf16[128,4096]{1,0:T(8,128)(2,1)}, bf16[128,4096]{1,0:T(8,128)(2,1)S(1)}, u32[]{:S(2)}, u32[]{:S(2)}) collective-permute-start(bf16[128,4096]{1,0:T(8,128)(2,1)} %slice.78), channel_id=1, source_target_pairs={{0,4},{4,0},{8,12},{12,8},{16,20},{20,16},{24,28},{28,24},{1,5},{5... | collective-permute-start | bytes 3145736 | tf_op jit(solution)/shard_map/ppermute | solution.py:225
  33.3 48.5 %collective-permute-start = (bf16[128,4096]{1,0:T(8,128)(2,1)}, bf16[128,4096]{1,0:T(8,128)(2,1)}, u32[]{:S(2)}, u32[]{:S(2)}) collective-permute-start(bf16[128,4096]{1,0:T(8,128)(2,1)} %slice.78), channel_id=1, source_target_pairs={{0,8},{4,12},{8,16},{12,20},{16,24},{20,28},{24,0},{28,4},{1,9},{5... | collective-permute-start | bytes 3145736 | tf_op jit(solution)/shard_map/ppermute | solution.py:225
  36.3 60.5 %collective-permute-start.5 = (f32[64,2048]{1,0:T(8,128)S(1)}, f32[64,2048]{1,0:T(8,128)}, u32[]{:S(2)}, u32[]{:S(2)}) collective-permute-start(f32[64,2048]{1,0:T(8,128)S(1)} %slice_add_fusion.10), channel_id=1, source_target_pairs={{0,2},{1,3},{2,0},{3,1},{4,6},{5,7},{6,4},{7,5},{8,10},{9,11},{10,... | collective-permute-start | bytes 1572872 | tf_op jit(solution)/shard_map/ppermute | solution.py:228
  59.3 41.3 %collective-permute-start.9 = (bf16[128,4096]{1,0:T(8,128)(2,1)S(1)}, bf16[128,4096]{1,0:T(8,128)(2,1)}, u32[]{:S(2)}, u32[]{:S(2)}) collective-permute-start(bf16[128,4096]{1,0:T(8,128)(2,1)S(1)} %collective-permute-done.6.refs_2_), channel_id=1, source_target_pairs={{0,4},{4,0},{8,12},{12,8},{16,20},{20,16},{24,28},{28,24},{1,5},{5... | collective-permute-start | bytes 3145736 | tf_op jit(solution)/shard_map/ppermute | solution.py:225
  59.5 44.8 %collective-permute-start.8 = (bf16[128,4096]{1,0:T(8,128)(2,1)S(1)}, bf16[128,4096]{1,0:T(8,128)(2,1)}, u32[]{:S(2)}, u32[]{:S(2)}) collective-permute-start(bf16[128,4096]{1,0:T(8,128)(2,1)S(1)} %collective-permute-done.6.refs_2_), channel_id=1, source_target_pairs={{0,8},{4,12},{8,16},{12,20},{16,24},{20,28},{24,0},{28,4},{1,9},{5... | collective-permute-start | bytes 3145736 | tf_op jit(solution)/shard_map/ppermute | solution.py:225
  81.8 41.0 %collective-permute-start.3 = (bf16[128,4096]{1,0:T(8,128)(2,1)}, bf16[128,4096]{1,0:T(8,128)(2,1)}, u32[]{:S(2)}, u32[]{:S(2)}) collective-permute-start(bf16[128,4096]{1,0:T(8,128)(2,1)} %collective-permute-done.refs_0_), channel_id=1, source_target_pairs={{0,4},{4,0},{8,12},{12,8},{16,20},{20,16},{24,28},{28,24},{1,5},{5... | collective-permute-start | bytes 3145736 | tf_op jit(solution)/shard_map/ppermute | solution.py:225
  82.1 44.0 %collective-permute-start.2 = (bf16[128,4096]{1,0:T(8,128)(2,1)}, bf16[128,4096]{1,0:T(8,128)(2,1)}, u32[]{:S(2)}, u32[]{:S(2)}) collective-permute-start(bf16[128,4096]{1,0:T(8,128)(2,1)} %collective-permute-done.refs_0_), channel_id=1, source_target_pairs={{0,8},{4,12},{8,16},{12,20},{16,24},{20,28},{24,0},{28,4},{1,9},{5... | collective-permute-start | bytes 3145736 | tf_op jit(solution)/shard_map/ppermute | solution.py:225
  96.8 53.5 %collective-permute-start.20 = (f32[256,2048]{1,0:T(8,128)}, f32[256,2048]{1,0:T(8,128)S(1)}, u32[]{:S(2)}, u32[]{:S(2)}) collective-permute-start(f32[256,2048]{1,0:T(8,128)} %get-tuple-element.56), channel_id=1, source_target_pairs={{0,1},{1,0},{2,3},{3,2},{4,5},{5,4},{6,7},{7,6},{8,9},{9,8},{10,11... | collective-permute-start | bytes 6291464 | tf_op jit(solution)/shard_map/ppermute | solution.py:228
  140.6 11.3 %collective-permute-start.12 = (f32[256,2048]{1,0:T(8,128)}, f32[256,2048]{1,0:T(8,128)S(1)}, u32[]{:S(2)}, u32[]{:S(2)}) collective-permute-start(f32[256,2048]{1,0:T(8,128)} %get-tuple-element.48), channel_id=1, source_target_pairs={{0,1},{1,0},{2,3},{3,2},{4,5},{5,4},{6,7},{7,6},{8,9},{9,8},{10,11... | collective-permute-start | bytes 6291464 | tf_op jit(solution)/shard_map/ppermute | solution.py:228
  149.7 29.1 %collective-permute-start.19 = (bf16[128,4096]{1,0:T(8,128)(2,1)}, bf16[128,4096]{1,0:T(8,128)(2,1)S(1)}, u32[]{:S(2)}, u32[]{:S(2)}) collective-permute-start(bf16[128,4096]{1,0:T(8,128)(2,1)} %collective-permute-done.2.refs_0_), channel_id=1, source_target_pairs={{0,4},{4,0},{8,12},{12,8},{16,20},{20,16},{24,28},{28,24},{1,5},{5... | collective-permute-start | bytes 3145736 | tf_op jit(solution)/shard_map/ppermute | solution.py:225
  150.3 31.0 %collective-permute-start.18 = (bf16[128,4096]{1,0:T(8,128)(2,1)}, bf16[128,4096]{1,0:T(8,128)(2,1)}, u32[]{:S(2)}, u32[]{:S(2)}) collective-permute-start(bf16[128,4096]{1,0:T(8,128)(2,1)} %collective-permute-done.2.refs_0_), channel_id=1, source_target_pairs={{0,8},{4,12},{8,16},{12,20},{16,24},{20,28},{24,0},{28,4},{1,9},{5... | collective-permute-start | bytes 3145736 | tf_op jit(solution)/shard_map/ppermute | solution.py:225
  150.4 26.1 %collective-permute-start.21 = (f32[128,2048]{1,0:T(8,128)S(1)}, f32[128,2048]{1,0:T(8,128)S(1)}, u32[]{:S(2)}, u32[]{:S(2)}) collective-permute-start(f32[128,2048]{1,0:T(8,128)S(1)} %slice_add_fusion), channel_id=1, source_target_pairs={{0,2},{1,3},{2,0},{3,1},{4,6},{5,7},{6,4},{7,5},{8,10},{9,11},{10,... | collective-permute-start | bytes 3145736 | tf_op jit(solution)/shard_map/ppermute | solution.py:228
  154.4 44.6 %collective-permute-start.13 = (f32[128,2048]{1,0:T(8,128)}, f32[128,2048]{1,0:T(8,128)}, u32[]{:S(2)}, u32[]{:S(2)}) collective-permute-start(f32[128,2048]{1,0:T(8,128)} %slice_add_fusion.2), channel_id=1, source_target_pairs={{0,2},{1,3},{2,0},{3,1},{4,6},{5,7},{6,4},{7,5},{8,10},{9,11},{10,... | collective-permute-start | bytes 3145736 | tf_op jit(solution)/shard_map/ppermute | solution.py:228
  155.8 47.2 %collective-permute-start.11 = (bf16[128,4096]{1,0:T(8,128)(2,1)}, bf16[128,4096]{1,0:T(8,128)(2,1)}, u32[]{:S(2)}, u32[]{:S(2)}) collective-permute-start(bf16[128,4096]{1,0:T(8,128)(2,1)} %collective-permute-done.8.refs_2_), channel_id=1, source_target_pairs={{0,4},{4,0},{8,12},{12,8},{16,20},{20,16},{24,28},{28,24},{1,5},{5... | collective-permute-start | bytes 3145736 | tf_op jit(solution)/shard_map/ppermute | solution.py:225
  176.5 28.0 %collective-permute-start.10 = (bf16[128,4096]{1,0:T(8,128)(2,1)}, bf16[128,4096]{1,0:T(8,128)(2,1)}, u32[]{:S(2)}, u32[]{:S(2)}) collective-permute-start(bf16[128,4096]{1,0:T(8,128)(2,1)} %collective-permute-done.8.refs_2_), channel_id=1, source_target_pairs={{0,8},{4,12},{8,16},{12,20},{16,24},{20,28},{24,0},{28,4},{1,9},{5... | collective-permute-start | bytes 3145736 | tf_op jit(solution)/shard_map/ppermute | solution.py:225
  179.8 39.2 %collective-permute-start.36 = (bf16[128,2048]{1,0:T(8,128)(2,1)S(1)}, bf16[128,2048]{1,0:T(8,128)(2,1)S(1)}, u32[]{:S(2)}, u32[]{:S(2)}) collective-permute-start(bf16[128,2048]{1,0:T(8,128)(2,1)S(1)} %get-tuple-element.72), channel_id=1, source_target_pairs={{0,2},{1,3},{2,0},{3,1},{4,6},{5,7},{6,4},{7,5},{8,10},{9,11},{10,... | collective-permute-start | bytes 1572872 | tf_op jit(solution)/shard_map/ppermute | solution.py:228
  191.8 28.9 %collective-permute-start.24 = (f32[128,2048]{1,0:T(8,128)}, f32[128,2048]{1,0:T(8,128)S(1)}, u32[]{:S(2)}, u32[]{:S(2)}) collective-permute-start(f32[128,2048]{1,0:T(8,128)} %get-tuple-element.61), channel_id=1, source_target_pairs={{0,1},{1,0},{2,3},{3,2},{4,5},{5,4},{6,7},{7,6},{8,9},{9,8},{10,11... | collective-permute-start | bytes 3145736 | tf_op jit(solution)/shard_map/ppermute | solution.py:228
  201.3 19.4 %collective-permute-start.30 = (bf16[128,2048]{1,0:T(8,128)(2,1)S(1)}, bf16[128,2048]{1,0:T(8,128)(2,1)S(1)}, u32[]{:S(2)}, u32[]{:S(2)}) collective-permute-start(bf16[128,2048]{1,0:T(8,128)(2,1)S(1)} %get-tuple-element.70), channel_id=1, source_target_pairs={{0,2},{1,3},{2,0},{3,1},{4,6},{5,7},{6,4},{7,5},{8,10},{9,11},{10,... | collective-permute-start | bytes 1572872 | tf_op jit(solution)/shard_map/ppermute | solution.py:228
  202.9 42.4 %collective-permute-start.22 = (bf16[128,4096]{1,0:T(8,128)(2,1)}, bf16[128,4096]{1,0:T(8,128)(2,1)S(1)}, u32[]{:S(2)}, u32[]{:S(2)}) collective-permute-start(bf16[128,4096]{1,0:T(8,128)(2,1)} %collective-permute-done.18.refs_0_), channel_id=1, source_target_pairs={{0,4},{4,0},{8,12},{12,8},{16,20},{20,16},{24,28},{28,24},{1,5},{5... | collective-permute-start | bytes 3145736 | tf_op jit(solution)/shard_map/ppermute | solution.py:225
  204.5 40.8 %collective-permute-start.23 = (bf16[128,4096]{1,0:T(8,128)(2,1)}, bf16[128,4096]{1,0:T(8,128)(2,1)S(1)}, u32[]{:S(2)}, u32[]{:S(2)}) collective-permute-start(bf16[128,4096]{1,0:T(8,128)(2,1)} %copy-done.5), channel_id=1, source_target_pairs={{0,24},{4,28},{8,0},{12,4},{16,8},{20,12},{24,16},{28,20},{1,25},{... | collective-permute-start | bytes 3145736 | tf_op jit(solution)/shard_map/ppermute | solution.py:225
  220.6 39.4 %collective-permute-start.37 = (bf16[256,2048]{1,0:T(8,128)(2,1)}, bf16[256,2048]{1,0:T(8,128)(2,1)}, u32[]{:S(2)}, u32[]{:S(2)}) collective-permute-start(bf16[256,2048]{1,0:T(8,128)(2,1)} %pad_maximum_fusion.3), channel_id=1, source_target_pairs={{0,1},{1,0},{2,3},{3,2},{4,5},{5,4},{6,7},{7,6},{8,9},{9,8},{10,11... | collective-permute-start | bytes 3145736 | tf_op jit(solution)/shard_map/ppermute | solution.py:228
  222.2 14.8 %collective-permute-start.25 = (f32[64,2048]{1,0:T(8,128)S(1)}, f32[64,2048]{1,0:T(8,128)S(1)}, u32[]{:S(2)}, u32[]{:S(2)}) collective-permute-start(f32[64,2048]{1,0:T(8,128)S(1)} %slice_add_fusion.6), channel_id=1, source_target_pairs={{0,2},{1,3},{2,0},{3,1},{4,6},{5,7},{6,4},{7,5},{8,10},{9,11},{10,... | collective-permute-start | bytes 1572872 | tf_op jit(solution)/shard_map/ppermute | solution.py:228
  224.8 37.6 %collective-permute-start.15 = (f32[64,2048]{1,0:T(8,128)}, f32[64,2048]{1,0:T(8,128)}, u32[]{:S(2)}, u32[]{:S(2)}) collective-permute-start(f32[64,2048]{1,0:T(8,128)} %slice_add_fusion.8), channel_id=1, source_target_pairs={{0,2},{1,3},{2,0},{3,1},{4,6},{5,7},{6,4},{7,5},{8,10},{9,11},{10,... | collective-permute-start | bytes 1572872 | tf_op jit(solution)/shard_map/ppermute | solution.py:228
  262.4 14.8 %collective-permute-start.32 = (bf16[64,2048]{1,0:T(8,128)(2,1)S(1)}, bf16[64,2048]{1,0:T(8,128)(2,1)S(1)}, u32[]{:S(2)}, u32[]{:S(2)}) collective-permute-start(bf16[64,2048]{1,0:T(8,128)(2,1)S(1)} %get-tuple-element.68), channel_id=1, source_target_pairs={{0,2},{1,3},{2,0},{3,1},{4,6},{5,7},{6,4},{7,5},{8,10},{9,11},{10,... | collective-permute-start | bytes 786440 | tf_op jit(solution)/shard_map/ppermute | solution.py:228
  263.5 13.6 %collective-permute-start.16 = (bf16[64,2048]{1,0:T(8,128)(2,1)S(1)}, bf16[64,2048]{1,0:T(8,128)(2,1)S(1)}, u32[]{:S(2)}, u32[]{:S(2)}) collective-permute-start(bf16[64,2048]{1,0:T(8,128)(2,1)S(1)} %fusion.16), channel_id=1, source_target_pairs={{0,2},{1,3},{2,0},{3,1},{4,6},{5,7},{6,4},{7,5},{8,10},{9,11},{10,... | collective-permute-start | bytes 786440 | tf_op jit(solution)/shard_map/ppermute | solution.py:228
  266.7 21.2 %collective-permute-start.27 = (f32[64,2048]{1,0:T(8,128)S(1)}, f32[64,2048]{1,0:T(8,128)S(1)}, u32[]{:S(2)}, u32[]{:S(2)}) collective-permute-start(f32[64,2048]{1,0:T(8,128)S(1)} %slice_add_fusion.4), channel_id=1, source_target_pairs={{0,2},{1,3},{2,0},{3,1},{4,6},{5,7},{6,4},{7,5},{8,10},{9,11},{10,... | collective-permute-start | bytes 1572872 | tf_op jit(solution)/shard_map/ppermute | solution.py:228
  277.1 29.3 %collective-permute-start.17 = (bf16[128,2048]{1,0:T(8,128)(2,1)S(1)}, bf16[128,2048]{1,0:T(8,128)(2,1)S(1)}, u32[]{:S(2)}, u32[]{:S(2)}) collective-permute-start(bf16[128,2048]{1,0:T(8,128)(2,1)S(1)} %pad_maximum_fusion.4), channel_id=1, source_target_pairs={{0,1},{1,0},{2,3},{3,2},{4,5},{5,4},{6,7},{7,6},{8,9},{9,8},{10,11... | collective-permute-start | bytes 1572872 | tf_op jit(solution)/shard_map/ppermute | solution.py:228
  277.3 12.2 %collective-permute-start.33 = (bf16[128,2048]{1,0:T(8,128)(2,1)S(1)}, bf16[128,2048]{1,0:T(8,128)(2,1)S(1)}, u32[]{:S(2)}, u32[]{:S(2)}) collective-permute-start(bf16[128,2048]{1,0:T(8,128)(2,1)S(1)} %pad_maximum_fusion.6), channel_id=1, source_target_pairs={{0,1},{1,0},{2,3},{3,2},{4,5},{5,4},{6,7},{7,6},{8,9},{9,8},{10,11... | collective-permute-start | bytes 1572872 | tf_op jit(solution)/shard_map/ppermute | solution.py:228
  297.2 10.4 %collective-permute-start.29 = (bf16[128,2048]{1,0:T(8,128)(2,1)S(1)}, bf16[128,2048]{1,0:T(8,128)(2,1)S(1)}, u32[]{:S(2)}, u32[]{:S(2)}) collective-permute-start(bf16[128,2048]{1,0:T(8,128)(2,1)S(1)} %pad_maximum_fusion.5), channel_id=1, source_target_pairs={{0,1},{1,0},{2,3},{3,2},{4,5},{5,4},{6,7},{7,6},{8,9},{9,8},{10,11... | collective-permute-start | bytes 1572872 | tf_op jit(solution)/shard_map/ppermute | solution.py:228
  (26 other events, 255.1 us)
Sparse Core Ops, SparseCore 0:
  203.0 107.0 all-gather.1
